TPU v7x, 32 devices: a whole 2x2x4 slice. The times are simulated.
32 devices in a mesh: tm: 16 (over z, y, core), batch: 2 (over x).
Axes of the slice: x: 2, y: 2, z: 4, core: 2. Of those that a mesh axis runs over, the one named last changes fastest.
Arguments:
- block_entry_input: bfloat16 [2, 8192, 384], P('batch', 'tm'), may hold values from -90 to 90
- prelude_output: bfloat16 [2, 8192, 256], P('batch', 'tm'), may hold values from -90 to 90
- leading_block_output: bfloat16 [2, 8192, 256], P('batch', 'tm'), may hold values from -90 to 90
- lengths: int32 [2, 16], P('batch'), may hold values from 1 to 1024, 8192 in all within a row
- leading_conv_weight: bfloat16 [512, 17, 384], replicated, may hold values from -0.078125 to 0.078125
- remaining_conv_weight: bfloat16 [4, 512, 17, 512], replicated, may hold values from -0.0625 to 0.0625
- gain: float32 [5, 512], replicated, may hold values from 0.25 to 1.75
- shift: float32 [5, 512], replicated, may hold values from -3 to 3
- residual_pointwise_weight: bfloat16 [512, 896], replicated, may hold values from -0.375 to 0.375
- residual_norm_scale: float32 [3, 512], replicated, may hold values from 0.4 to 0.8
- residual_norm_bias: float32 [3, 512], replicated, may hold values from -3 to 3
- cotangent: bfloat16 [2, 8192, 512], P('batch', 'tm'), may hold values from -90 to 90
Outputs:
- block_output: bfloat16 [2, 8192, 512], P('batch', 'tm')
- grad_block_input: bfloat16 [2, 8192, 384], P('batch', 'tm')
- prelude_gradient: bfloat16 [2, 8192, 256], P('batch', 'tm')
- grad_first: bfloat16 [2, 8192, 256], P('batch', 'tm')
- grad_w_first: float32 [512, 17, 384], P('tm')
- grad_w_rest: float32 [4, 512, 17, 512], P(None, 'tm')
- grad_gain: float32 [5, 512], P(None, 'tm')
- grad_shift: float32 [4, 512], P(None, 'tm')
- grad_last_shift: float32 [512], P('tm')
- grad_res_weight: float32 [512, 896], P('tm')
- grad_res_gain: float32 [3, 512], P(None, 'tm')
- grad_res_shift: float32 [3, 512], P(None, 'tm')
Inputs may be any that keep to these rules, and one draw needn't show every extreme that they name: Each row's 16 utterance lengths sum to 8192, and the longest is exactly 1024.
All inputs are finite; a program needn't handle non-finite values.
Results may differ from a plain program's by a relative error of at most 0.023.
Values may be sent and summed in bfloat16 or wider, within the bound.
No kernel may reach another device: no remote copies, remote signals or barrier semaphores. Data moves between devices by JAX's collectives and lax.ppermute only.
A program may use at most 256 MiB of HBM per device.

v0:
```python
import jax
import jax.numpy as jnp
from jax import lax
from jax.sharding import PartitionSpec as P

norm_eps = 0.001


def with_halo(block, sides, width):
    for axis, dim in sides:
        count = lax.axis_size(axis)
        forward = [(i, i + 1) for i in range(count - 1)]
        backward = [(target, source) for source, target in forward]
        low = lax.ppermute(
            lax.slice_in_dim(block, block.shape[dim] - width, None, axis=dim), axis, forward
        )
        high = lax.ppermute(lax.slice_in_dim(block, 0, width, axis=dim), axis, backward)
        block = jnp.concatenate([low, block, high], axis=dim)
    return block


def smooth(values):
    return values * jax.nn.sigmoid(values)


def smooth_slope(values):
    squashed = jax.nn.sigmoid(values)
    return squashed * (1.0 + values * (1.0 - squashed))


def unfold(padded, tap_mask, frames, tap_order):
    stacked = jnp.stack([padded[start_row : start_row + frames] for start_row in tap_order], axis=1)
    return stacked * tap_mask[:, :, None]


def per_device(
    block_entry_input,
    prelude_output,
    leading_block_output,
    lengths,
    leading_conv_weight,
    remaining_conv_weight,
    gain,
    shift,
    residual_pointwise_weight,
    residual_norm_scale,
    residual_norm_bias,
    cotangent,
):
    frames = block_entry_input.shape[1]
    channels = leading_conv_weight.shape[0]
    kernel_taps = leading_conv_weight.shape[1]
    margin = kernel_taps // 2
    layers = remaining_conv_weight.shape[0] + 1
    tm_count = lax.axis_size("tm")
    tm_place = lax.axis_index("tm")
    row_frames = frames * tm_count
    samples = float(row_frames * lax.axis_size("batch") * block_entry_input.shape[0])
    row_lengths = lengths[0]
    starts = jnp.cumsum(row_lengths) - row_lengths
    position = tm_place * frames - margin + jnp.arange(frames + 2 * margin, dtype=jnp.int32)
    segment = jnp.sum((position[:, None] >= starts[None, :]).astype(jnp.int32), axis=1) - 1
    segment = jnp.where(position < row_frames, segment, -1)
    centre = segment[margin : margin + frames]
    ahead_mask = jnp.stack(
        [segment[start_row : start_row + frames] == centre for start_row in range(kernel_taps)],
        axis=1,
    ).astype(jnp.bfloat16)
    behind_mask = ahead_mask[:, ::-1]
    ahead_order = list(range(kernel_taps))
    behind_order = ahead_order[::-1]

    def normalize(values, total_first, total_second):
        average = total_first / samples
        inv_std = lax.rsqrt(total_second / samples - average * average + norm_eps)
        return ((values - average) * inv_std, inv_std)

    def norm_back(grad_out, normed, inv_std, scale, total_shift, total_gain):
        return (
            scale * inv_std * (grad_out - total_shift / samples - normed * total_gain / samples)
        ).astype(jnp.bfloat16)

    source_arrays = (prelude_output[0], leading_block_output[0], block_entry_input[0])
    bounds = [
        0,
        source_arrays[0].shape[1],
        source_arrays[0].shape[1] + source_arrays[1].shape[1],
        residual_pointwise_weight.shape[1],
    ]
    res_parts = [
        residual_pointwise_weight[:, bounds[branch] : bounds[branch + 1]] for branch in range(3)
    ]
    res_conv = [
        lax.dot_general(
            source_arrays[branch],
            res_parts[branch],
            (((1,), (1,)), ((), ())),
            preferred_element_type=jnp.float32,
        )
        for branch in range(3)
    ]
    res_first = jnp.concatenate([jnp.sum(values, axis=0) for values in res_conv])
    res_second = jnp.concatenate([jnp.sum(values * values, axis=0) for values in res_conv])
    res_total_first, res_total_second = lax.psum((res_first, res_second), ("tm", "batch"))
    current = block_entry_input[0]
    stored = []
    for layer in range(layers):
        weight = leading_conv_weight if layer == 0 else remaining_conv_weight[layer - 1]
        padded = with_halo(current[None], (("tm", 1),), margin)[0]
        columns = unfold(padded, ahead_mask, frames, ahead_order)
        conv_out = lax.dot_general(
            columns, weight, (((1, 2), (1, 2)), ((), ())), preferred_element_type=jnp.float32
        )
        first_sum = jnp.sum(conv_out, axis=0)
        second_sum = jnp.sum(conv_out * conv_out, axis=0)
        total_first, total_second = lax.psum((first_sum, second_sum), ("tm", "batch"))
        normed, inv_std = normalize(conv_out, total_first, total_second)
        pre_act = normed * gain[layer] + shift[layer]
        stored.append((columns, normed, inv_std, pre_act))
        if layer < layers - 1:
            current = smooth(pre_act).astype(jnp.bfloat16)
    res_normed = []
    residual = jnp.zeros_like(pre_act)
    for branch in range(3):
        window = slice(branch * channels, (branch + 1) * channels)
        normed, inv_std = normalize(
            res_conv[branch], res_total_first[window], res_total_second[window]
        )
        res_normed.append((normed, inv_std))
        residual = residual + normed * residual_norm_scale[branch] + residual_norm_bias[branch]
    joined = pre_act + residual
    block_output = smooth(joined).astype(jnp.bfloat16)
    grad_pre = cotangent[0].astype(jnp.float32) * smooth_slope(joined)
    gain_grads = [None] * layers
    shift_grads = [None] * layers
    weight_terms = [None] * layers
    for layer in reversed(range(layers)):
        columns, normed, inv_std, pre_act = stored[layer]
        weight = leading_conv_weight if layer == 0 else remaining_conv_weight[layer - 1]
        shift_sum = jnp.sum(grad_pre, axis=0)
        gain_sum = jnp.sum(grad_pre * normed, axis=0)
        if layer == layers - 1:
            gain_sum = jnp.concatenate(
                [gain_sum] + [jnp.sum(grad_pre * entry[0], axis=0) for entry in res_normed]
            )
        total_shift, total_gain = lax.psum((shift_sum, gain_sum), ("tm", "batch"))
        shift_grads[layer] = total_shift
        gain_grads[layer] = total_gain[:channels]
        if layer == layers - 1:
            res_gain_grads = [
                total_gain[(branch + 1) * channels : (branch + 2) * channels] for branch in range(3)
            ]
            res_shift_grad = total_shift
            res_low = [
                norm_back(
                    grad_pre,
                    res_normed[branch][0],
                    res_normed[branch][1],
                    residual_norm_scale[branch],
                    total_shift,
                    res_gain_grads[branch],
                )
                for branch in range(3)
            ]
            res_term = jnp.concatenate(
                [
                    lax.dot_general(
                        res_low[branch],
                        source_arrays[branch],
                        (((0,), (0,)), ((), ())),
                        preferred_element_type=jnp.float32,
                    )
                    for branch in range(3)
                ],
                axis=1,
            )
            residual_input_list = [
                jnp.dot(res_low[branch], res_parts[branch], preferred_element_type=jnp.float32)
                for branch in range(3)
            ]
        grad_low = norm_back(
            grad_pre, normed, inv_std, gain[layer], total_shift, total_gain[:channels]
        )
        weight_term = lax.dot_general(
            grad_low, columns, (((0,), (0,)), ((), ())), preferred_element_type=jnp.float32
        )
        weight_terms[layer] = weight_term
        grad_padded = with_halo(grad_low[None], (("tm", 1),), margin)[0]
        back_columns = unfold(grad_padded, behind_mask, frames, behind_order)
        grad_input = lax.dot_general(
            back_columns, weight, (((1, 2), (1, 0)), ((), ())), preferred_element_type=jnp.float32
        )
        if layer > 0:
            grad_pre = grad_input * smooth_slope(stored[layer - 1][3])
    summed = (
        lax.psum_scatter(
            weight_terms[0].astype(jnp.bfloat16), "tm", scatter_dimension=0, tiled=True
        ).astype(jnp.float32),
        lax.psum_scatter(
            weight_terms[1].astype(jnp.bfloat16), "tm", scatter_dimension=0, tiled=True
        ).astype(jnp.float32),
        lax.psum_scatter(
            weight_terms[2].astype(jnp.bfloat16), "tm", scatter_dimension=0, tiled=True
        ).astype(jnp.float32),
        lax.psum_scatter(
            weight_terms[3].astype(jnp.bfloat16), "tm", scatter_dimension=0, tiled=True
        ).astype(jnp.float32),
        lax.psum_scatter(
            weight_terms[4].astype(jnp.bfloat16), "tm", scatter_dimension=0, tiled=True
        ).astype(jnp.float32),
        lax.psum_scatter(
            res_term.astype(jnp.bfloat16), "tm", scatter_dimension=0, tiled=True
        ).astype(jnp.float32),
    )
    results = (
        lax.psum(summed[0].astype(jnp.bfloat16), "batch").astype(jnp.float32),
        lax.psum(summed[1].astype(jnp.bfloat16), "batch").astype(jnp.float32),
        lax.psum(summed[2].astype(jnp.bfloat16), "batch").astype(jnp.float32),
        lax.psum(summed[3].astype(jnp.bfloat16), "batch").astype(jnp.float32),
        lax.psum(summed[4].astype(jnp.bfloat16), "batch").astype(jnp.float32),
        lax.psum(summed[5].astype(jnp.bfloat16), "batch").astype(jnp.float32),
    )
    width_dev = channels // tm_count

    def local_share(vector_sum):
        return lax.dynamic_slice_in_dim(vector_sum, tm_place * width_dev, width_dev)

    grad_gain = jnp.stack([local_share(vector_sum) for vector_sum in gain_grads])
    grad_shift = jnp.stack([local_share(vector_sum) for vector_sum in shift_grads[: layers - 1]])
    grad_last_shift = local_share(shift_grads[layers - 1])
    grad_res_gain = jnp.stack([local_share(vector_sum) for vector_sum in res_gain_grads])
    grad_res_shift = jnp.stack([local_share(res_shift_grad) for branch in range(3)])
    grad_block_input = (grad_input + residual_input_list[2]).astype(jnp.bfloat16)[None]
    prelude_gradient = residual_input_list[0].astype(jnp.bfloat16)[None]
    grad_first = residual_input_list[1].astype(jnp.bfloat16)[None]
    grad_w_first = results[0]
    grad_w_rest = jnp.stack([results[1], results[2], results[3], results[4]])
    grad_res_weight = results[5]
    return (
        block_output[None],
        grad_block_input,
        prelude_gradient,
        grad_first,
        grad_w_first,
        grad_w_rest,
        grad_gain,
        grad_shift,
        grad_last_shift,
        grad_res_weight,
        grad_res_gain,
        grad_res_shift,
    )


def solution(mesh):
    in_specs = (
        P("batch", "tm", None),
        P("batch", "tm", None),
        P("batch", "tm", None),
        P("batch", None),
        P(),
        P(),
        P(),
        P(),
        P(),
        P(),
        P(),
        P("batch", "tm", None),
    )
    out_specs = (
        P("batch", "tm", None),
        P("batch", "tm", None),
        P("batch", "tm", None),
        P("batch", "tm", None),
        P("tm", None, None),
        P(None, "tm", None, None),
        P(None, "tm"),
        P(None, "tm"),
        P("tm"),
        P("tm", None),
        P(None, "tm"),
        P(None, "tm"),
    )
    return jax.shard_map(
        per_device, mesh=mesh, in_specs=in_specs, out_specs=out_specs, check_vma=False
    )
```

profile of v0, /device:TPU:0, one launch (start us, length us, event | category | flops | bytes accessed | tf_op | source)
XLA Modules:
  0.0 1363.9 jit_solution(18364115657844031977)
XLA Ops:
  9.3 3.0 collective-permute-start
  15.9 3.1 fusion.618
  24.1 9.1 fusion.622
  33.2 42.4 %all-reduce.9 = (f32[512]{0:T(512)S(1)}, f32[512]{0:T(512)S(1)}) all-reduce(f32[512]{0:T(512)S(1)} %get-tuple-element.76, f32[512]{0:T(512)S(1)} %get-tuple-element.75), channel_id=1, replica_groups=mesh['tm'=16,'batch'=2] {'tm','batch'}, use_global_device_ids=true, to_apply=%region_5.6 | all-reduce | flops 1024 | bytes 8192 | tf_op jit(solution)/shard_map/psum | solution.py:116
  77.9 2.3 fusion.617
  97.6 10.9 fusion.621
  108.5 43.0 %all-reduce.8 = (f32[512]{0:T(512)S(1)}, f32[512]{0:T(512)S(1)}) all-reduce(f32[512]{0:T(512)S(1)} %get-tuple-element.74, f32[512]{0:T(512)S(1)} %get-tuple-element.73), channel_id=1, replica_groups=mesh['tm'=16,'batch'=2] {'tm','batch'}, use_global_device_ids=true, to_apply=%region_9.10 | all-reduce | flops 1024 | bytes 8192 | tf_op jit(solution)/shard_map/psum | solution.py:116
  171.2 10.9 fusion.620
  182.1 43.9 %all-reduce.7 = (f32[512]{0:T(512)S(1)}, f32[512]{0:T(512)S(1)}) all-reduce(f32[512]{0:T(512)S(1)} %get-tuple-element.72, f32[512]{0:T(512)S(1)} %get-tuple-element.71), channel_id=1, replica_groups=mesh['tm'=16,'batch'=2] {'tm','batch'}, use_global_device_ids=true, to_apply=%region_13.14 | all-reduce | flops 1024 | bytes 8192 | tf_op jit(solution)/shard_map/psum | solution.py:116
  246.5 10.9 fusion.619
  257.5 43.1 %all-reduce.6 = (f32[512]{0:T(512)S(1)}, f32[512]{0:T(512)S(1)}) all-reduce(f32[512]{0:T(512)S(1)} %get-tuple-element.70, f32[512]{0:T(512)S(1)} %get-tuple-element.69), channel_id=1, replica_groups=mesh['tm'=16,'batch'=2] {'tm','batch'}, use_global_device_ids=true, to_apply=%region_17.18 | all-reduce | flops 1024 | bytes 8192 | tf_op jit(solution)/shard_map/psum | solution.py:116
  320.8 11.8 fusion.615
  332.7 44.0 %all-reduce.5 = (f32[1536]{0:T(1024)S(1)}, f32[1536]{0:T(1024)S(1)}, f32[512]{0:T(512)S(1)}, f32[512]{0:T(512)S(1)}) all-reduce(f32[1536]{0:T(1024)S(1)} %get-tuple-element.204, f32[1536]{0:T(1024)S(1)} %get-tuple-element.203, f32[512]{0:T(512)S(1)} %get-tuple-element.62, ...), channel_id=1, replica_groups=mesh['tm'=16,'batch'=2] {'tm','batch'}, use_global_device_ids=true, to_apply=%region_29.30 | all-reduce | flops 4096 | bytes 32768 | tf_op jit(solution)/shard_map/psum | solution.py:104
  377.9 4.3 fusion.614
  382.2 40.3 %all-reduce.4 = (f32[2048]{0:T(1024)S(1)}, f32[512]{0:T(512)S(1)}) all-reduce(f32[2048]{0:T(1024)S(1)} %pad_maximum_fusion.21, f32[512]{0:T(512)S(1)} %get-tuple-element.56), channel_id=1, replica_groups=mesh['tm'=16,'batch'=2] {'tm','batch'}, use_global_device_ids=true, to_apply=%region_36.37 | all-reduce | flops 2560 | bytes 20480 | tf_op jit(solution)/shard_map/psum | solution.py:146
  423.1 3.6 multiply_convert_fusion
  428.2 3.4 collective-permute-start.11
  433.6 9.7 fusion.613
  443.4 41.7 %all-reduce.3 = (f32[512]{0:T(512)S(1)}, f32[512]{0:T(512)S(1)}) all-reduce(f32[512]{0:T(512)S(1)} %get-tuple-element.55, f32[512]{0:T(512)S(1)} %get-tuple-element.54), channel_id=1, replica_groups=mesh['tm'=16,'batch'=2] {'tm','batch'}, use_global_device_ids=true, to_apply=%region_40.41 | all-reduce | flops 1024 | bytes 8192 | tf_op jit(solution)/shard_map/psum | solution.py:146
  488.0 3.4 collective-permute-start.13
  493.4 9.7 fusion.612
  503.1 42.7 %all-reduce.2 = (f32[512]{0:T(512)S(1)}, f32[512]{0:T(512)S(1)}) all-reduce(f32[512]{0:T(512)S(1)} %get-tuple-element.53, f32[512]{0:T(512)S(1)} %get-tuple-element.52), channel_id=1, replica_groups=mesh['tm'=16,'batch'=2] {'tm','batch'}, use_global_device_ids=true, to_apply=%region_44.45 | all-reduce | flops 1024 | bytes 8192 | tf_op jit(solution)/shard_map/psum | solution.py:146
  549.0 3.5 collective-permute-start.15
  554.5 9.7 fusion.611
  564.2 40.8 %all-reduce.1 = (f32[512]{0:T(512)S(1)}, f32[512]{0:T(512)S(1)}) all-reduce(f32[512]{0:T(512)S(1)} %get-tuple-element.51, f32[512]{0:T(512)S(1)} %get-tuple-element.50), channel_id=1, replica_groups=mesh['tm'=16,'batch'=2] {'tm','batch'}, use_global_device_ids=true, to_apply=%region_48.49 | all-reduce | flops 1024 | bytes 8192 | tf_op jit(solution)/shard_map/psum | solution.py:146
  608.1 3.3 collective-permute-start.17
  613.5 9.7 fusion.610
  623.2 42.6 %all-reduce = (f32[512]{0:T(512)S(1)}, f32[512]{0:T(512)S(1)}) all-reduce(f32[512]{0:T(512)S(1)} %get-tuple-element.49, f32[512]{0:T(512)S(1)} %get-tuple-element.48), channel_id=1, replica_groups=mesh['tm'=16,'batch'=2] {'tm','batch'}, use_global_device_ids=true, to_apply=%region_52.53 | all-reduce | flops 1024 | bytes 8192 | tf_op jit(solution)/shard_map/psum | solution.py:146
  667.6 8.1 convolution_convert_fusion
  675.8 9.9 fusion.51
  686.0 10.2 fusion.48
  696.2 10.0 fusion.45
  706.3 10.1 fusion.42
  724.2 2.1 fusion.141
  728.3 2.4 fusion.561
  737.0 2.2 collective-permute-done.18
  745.5 18.2 %reduce-scatter.9.cloned.1.call-done = bf16[32,17,384]{2,0,1:T(8,128)(2,1)} async-done(((bf16[512,17,384]{2,0,1:T(8,128)(2,1)}), bf16[32,17,384]{2,0,1:T(8,128)(2,1)}) %reduce-scatter.9.cloned.1.call-update) | async-done | bytes 417808 | tf_op jit(solution)/shard_map/reduce_scatter | solution.py:196
  763.7 111.1 %reduce-scatter.17.cloned.1.call-done = bf16[32,17,512]{2,0,1:T(8,128)(2,1)} async-done(((bf16[512,17,512]{2,0,1:T(8,128)(2,1)}), bf16[32,17,512]{2,0,1:T(8,128)(2,1)}) %reduce-scatter.17.cloned.1.call-update) | async-done | bytes 557072 | tf_op jit(solution)/shard_map/reduce_scatter | solution.py:208
  874.7 112.2 %reduce-scatter.15.cloned.1.call-done = bf16[32,17,512]{2,0,1:T(8,128)(2,1)} async-done(((bf16[512,17,512]{2,0,1:T(8,128)(2,1)}), bf16[32,17,512]{2,0,1:T(8,128)(2,1)}) %reduce-scatter.15.cloned.1.call-update) | async-done | bytes 557072 | tf_op jit(solution)/shard_map/reduce_scatter | solution.py:205
  987.0 111.5 %reduce-scatter.13.cloned.1.call-done = bf16[32,17,512]{2,0,1:T(8,128)(2,1)} async-done(((bf16[512,17,512]{2,0,1:T(8,128)(2,1)}), bf16[32,17,512]{2,0,1:T(8,128)(2,1)}) %reduce-scatter.13.cloned.1.call-update) | async-done | bytes 557072 | tf_op jit(solution)/shard_map/reduce_scatter | solution.py:202
  1098.5 112.1 %reduce-scatter.11.cloned.1.call-done = bf16[32,17,512]{2,0,1:T(8,128)(2,1)} async-done(((bf16[512,17,512]{2,0,1:T(8,128)(2,1)}), bf16[32,17,512]{2,0,1:T(8,128)(2,1)}) %reduce-scatter.11.cloned.1.call-update) | async-done | bytes 557072 | tf_op jit(solution)/shard_map/reduce_scatter | solution.py:199
  1219.7 9.6 fusion.135
  1229.3 2.2 fusion.139
  1231.5 39.9 %reduce-scatter.19.cloned.1.call-done = bf16[32,896]{1,0:T(8,128)(2,1)} async-done(((bf16[512,896]{1,0:T(8,128)(2,1)}), bf16[32,896]{1,0:T(8,128)(2,1)}) %reduce-scatter.19.cloned.1.call-update) | async-done | bytes 57360
  1272.4 13.7 %psum.223 = bf16[32,896]{0,1:T(8,128)(2,1)S(1)} all-reduce(bf16[32,896]{0,1:T(8,128)(2,1)S(1)} %copy.53), channel_id=1, replica_groups=mesh['tm'=16,'batch'=2] {'batch'}, use_global_device_ids=true, to_apply=%region_64.65 | all-reduce | flops 28672 | bytes 114688 | tf_op jit(solution)/shard_map/psum | solution.py:221
  1286.8 63.2 %all-reduce.13.cloned.1.call-done = (bf16[32,17,384]{2,0,1:T(8,128)(2,1)}, bf16[1,32,17,512]{3,1,2,0:T(8,128)(2,1)}, bf16[1,32,17,512]{3,1,2,0:T(8,128)(2,1)}, b...) async-done(((bf16[32,17,384]{2,0,1:T(8,128)(2,1)}, bf16[1,32,17,512]{3,1,2,0:T(8,128)(2,1)}, bf16[1,32,17,512]{3,1,2,0:T(8,128)(2,1)}, ...) | async-done | bytes 2646032 | tf_op jit(solution)/shard_map/psum | solution.py:216
  1350.0 2.0 convert_element_type.123
  1352.0 4.0 maximum_convert_fusion
  (371 shorter events, 146.3 us)
Async XLA Ops:
  7.2 70.7 %copy-start = (bf16[1,512,256]{2,1,0:T(8,128)(2,1)S(1)}, bf16[1,512,256]{2,1,0:T(8,128)(2,1)}, u32[]{:S(2)}) copy-start(bf16[1,512,256]{2,1,0:T(8,128)(2,1)} %param.14) | copy-start | bytes 786436
  7.2 15.8 %copy-start.15 = (bf16[1,512,384]{2,1,0:T(8,128)(2,1)S(1)}, bf16[1,512,384]{2,1,0:T(8,128)(2,1)}, u32[]{:S(2)}) copy-start(bf16[1,512,384]{2,1,0:T(8,128)(2,1)} %param.12) | copy-start | bytes 1179652
  7.2 756.5 %reduce-scatter.9.cloned.1.call-start = ((), (), s32[]{:S(2)}) async-start(), calls=%async_computation.6 | async-start | bytes 7102464 | tf_op jit(solution)/shard_map/reduce_scatter | solution.py:196
  8.0 15.0 %collective-permute-start.1 = (bf16[1,8,384]{2,1,0:T(8,128)(2,1)S(1)}, bf16[1,8,384]{2,1,0:T(8,128)(2,1)S(1)}, u32[]{:S(2)}, u32[]{:S(2)}) collective-permute-start(bf16[1,8,384]{2,1,0:T(8,128)(2,1)S(1)} %get-tuple-element.127), channel_id=1, source_target_pairs={{2,0},{4,2},{6,4},{8,6},{10,8},{12,10},{14,12},{16,14},{18,16},{20... | collective-permute-start | bytes 18440 | tf_op jit(solution)/shard_map/ppermute | solution.py:17
  9.3 11.5 collective-permute-start
  20.4 357.5 %copy-start.1 = (f32[512,512]{1,0:T(8,128)}, f32[512,512]{1,0:T(8,128)S(1)}, u32[]{:S(2)}) copy-start(f32[512,512]{1,0:T(8,128)S(1)} %get-tuple-element.193) | copy-start | bytes 3145732
  24.1 9.1 copy-start.16
  33.2 61.7 %copy-start.3 = (f32[512,512]{1,0:T(8,128)}, f32[512,512]{1,0:T(8,128)S(1)}, u32[]{:S(2)}) copy-start(f32[512,512]{1,0:T(8,128)S(1)} %get-tuple-element.194) | copy-start | bytes 3145732
  76.6 5.2 collective-permute-start.2
  80.3 10.0 collective-permute-start.3
  97.6 56.2 %copy-start.25 = (f32[3,512]{1,0:T(4,128)S(1)}, f32[3,512]{1,0:T(4,128)}, u32[]{:S(2)}) copy-start(f32[3,512]{1,0:T(4,128)} %param.21) | copy-start | bytes 18436
  108.5 446.0 %copy-start.5 = (f32[512,512]{1,0:T(8,128)}, f32[512,512]{1,0:T(8,128)S(1)}, u32[]{:S(2)}) copy-start(f32[512,512]{1,0:T(8,128)S(1)} %get-tuple-element.195) | copy-start | bytes 3145732
  152.5 2.9 collective-permute-start.4
  153.8 10.1 collective-permute-start.5
  171.2 57.0 %copy-start.26 = (f32[3,512]{1,0:T(4,128)S(1)}, f32[3,512]{1,0:T(4,128)}, u32[]{:S(2)}) copy-start(f32[3,512]{1,0:T(4,128)} %param.22) | copy-start | bytes 18436
  182.1 62.6 %copy-start.8 = (f32[512,512]{1,0:T(8,128)}, f32[512,512]{1,0:T(8,128)S(1)}, u32[]{:S(2)}) copy-start(f32[512,512]{1,0:T(8,128)S(1)} %get-tuple-element.196) | copy-start | bytes 3145732
  226.9 3.7 collective-permute-start.6
  228.8 10.3 collective-permute-start.7
  257.4 61.6 %copy-start.10 = (f32[512,512]{1,0:T(8,128)}, f32[512,512]{1,0:T(8,128)S(1)}, u32[]{:S(2)}) copy-start(f32[512,512]{1,0:T(8,128)S(1)} %get-tuple-element.197) | copy-start | bytes 3145732
  301.5 3.5 collective-permute-start.8
  303.5 10.1 collective-permute-start.9
  382.2 50.8 %copy-start.6 = (f32[512,512]{1,0:T(8,128)}, f32[512,512]{1,0:T(8,128)S(1)}, u32[]{:S(2)}) copy-start(f32[512,512]{1,0:T(8,128)S(1)} %get-tuple-element.104) | copy-start | bytes 3145732
  426.7 4.9 collective-permute-start.10
  428.2 5.4 copy-start.11
  428.2 4.4 collective-permute-start.11
  433.6 51.5 %copy-start.12 = (f32[512,512]{1,0:T(8,128)S(1)}, f32[512,512]{1,0:T(8,128)}, u32[]{:S(2)}) copy-start(f32[512,512]{1,0:T(8,128)} %copy-done.10) | copy-start | bytes 3145732
  433.6 51.5 %copy-start.23 = (f32[512]{0:T(512)S(1)}, f32[512]{0:T(512)}, u32[]{:S(2)}) copy-start(f32[512]{0:T(512)} %get-tuple-element.166) | copy-start | bytes 6148
  486.6 4.7 collective-permute-start.12
  487.9 5.5 copy-start.9
  488.0 4.5 collective-permute-start.13
  493.4 52.4 %copy-start.22 = (f32[512]{0:T(512)S(1)}, f32[512]{0:T(512)}, u32[]{:S(2)}) copy-start(f32[512]{0:T(512)} %get-tuple-element.164) | copy-start | bytes 6148
  547.7 4.8 collective-permute-start.14
  549.0 4.5 collective-permute-start.15
  554.5 50.5 %copy-start.21 = (f32[512]{0:T(512)S(1)}, f32[512]{0:T(512)}, u32[]{:S(2)}) copy-start(f32[512]{0:T(512)} %get-tuple-element.162) | copy-start | bytes 6148
  606.8 4.7 collective-permute-start.16
  608.1 5.4 copy-start.4
  608.1 4.4 collective-permute-start.17
  613.5 52.3 %copy-start.20 = (f32[512]{0:T(512)S(1)}, f32[512]{0:T(512)}, u32[]{:S(2)}) copy-start(f32[512]{0:T(512)} %get-tuple-element.160) | copy-start | bytes 6148
  675.8 199.0 %reduce-scatter.17.cloned.1.call-start = ((), (), s32[]{:S(2)}) async-start(), calls=%async_computation.10 | async-start | bytes 9469952 | tf_op jit(solution)/shard_map/reduce_scatter | solution.py:208
  685.7 301.3 %reduce-scatter.15.cloned.1.call-start = ((), (), s32[]{:S(2)}) async-start(), calls=%async_computation.9 | async-start | bytes 9469952 | tf_op jit(solution)/shard_map/reduce_scatter | solution.py:205
  696.2 402.3 %reduce-scatter.13.cloned.1.call-start = ((), (), s32[]{:S(2)}) async-start(), calls=%async_computation.8 | async-start | bytes 9469952 | tf_op jit(solution)/shard_map/reduce_scatter | solution.py:202
  706.2 504.4 %reduce-scatter.11.cloned.1.call-start = ((), (), s32[]{:S(2)}) async-start(), calls=%async_computation.7 | async-start | bytes 9469952 | tf_op jit(solution)/shard_map/reduce_scatter | solution.py:199
  716.4 555.0 %reduce-scatter.19.cloned.1.call-start = ((), (), s32[]{:S(2)}) async-start(), calls=%async_computation.11 | async-start | bytes 974848
  717.3 638.7 %copy-start.29 = (f32[32]{0:T(128)}, f32[32]{0:T(128)S(1)}, u32[]{:S(2)}) copy-start(f32[32]{0:T(128)S(1)} %dynamic_slice.51) | copy-start | bytes 388
  730.7 619.4 %all-reduce.13.cloned.1.call-start = ((), (), s32[]{:S(2)}) async-start(), calls=%async_computation.12 | async-start | bytes 5292032 | tf_op jit(solution)/shard_map/psum | solution.py:216
  732.4 479.9 %collective-permute-start.19 = (bf16[1,8,512]{2,1,0:T(8,128)(2,1)S(1)}, bf16[1,8,512]{2,1,0:T(8,128)(2,1)S(1)}, u32[]{:S(2)}, u32[]{:S(2)}) collective-permute-start(bf16[1,8,512]{2,1,0:T(8,128)(2,1)S(1)} %get-tuple-element.109), channel_id=1, source_target_pairs={{0,2},{2,4},{4,6},{6,8},{8,10},{10,12},{12,14},{14,16},{16,18},{18... | collective-permute-start | bytes 24584 | tf_op jit(solution)/shard_map/ppermute | solution.py:14
  734.0 5.1 collective-permute-start.18
  1219.7 9.6 copy-start.14
  (9 other events, 16.9 us)
Sparse Core Ops, SparseCore 0:
  675.9 87.7 reduce-scatter.8
  767.8 106.9 reduce-scatter.16
  879.4 107.5 reduce-scatter.14
  990.9 107.5 reduce-scatter.12
  1103.0 107.5 reduce-scatter.10
  1214.6 56.7 reduce-scatter.18
  1274.2 75.8 all-reduce.12
where the time goes:
time: 1370 us; the launch traced here: 1360 us
  waiting for transfers between devices  571 us (42%)
  blocking collectives  438 us (32%)
  matrix products  166 us (12%)
  other arithmetic  118 us (9%)
  starting transfers between devices  38.1 us (3%)
  local copies, waits for them, and re-layouts  16.8 us (1%)
  between operations  16.1 us (1%)
    psum x5, blocking collectives, per_device(): total_shift, total_gain = lax.psum((shift_sum, gain_sum), ('tm', 'batch'))  208 us
    psum x4, blocking collectives, per_device(): lax.psum((first_sum, second_sum), ('tm', 'batch'))  172 us
    reduce_scatter x1, waiting for transfers between devices, per_device(): lax.psum_scatter(weight_terms[3].astype(jnp.bfloat16), 'tm', scatter_dime...  112 us
    reduce_scatter x1, waiting for transfers between devices, per_device(): lax.psum_scatter(weight_terms[1].astype(jnp.bfloat16), 'tm', scatter_dime...  112 us
    reduce_scatter x1, waiting for transfers between devices, per_device(): lax.psum_scatter(weight_terms[2].astype(jnp.bfloat16), 'tm', scatter_dime...  112 us
    reduce_scatter x1, waiting for transfers between devices, per_device(): lax.psum_scatter(weight_terms[4].astype(jnp.bfloat16), 'tm', scatter_dime...  111 us
    unnamed x139, other arithmetic  81.1 us
    psum x1, waiting for transfers between devices, per_device(): lax.psum(summed[0].astype(jnp.bfloat16), 'batch').astype(jnp.float32)  63.2 us
  transfers between devices with their start and end apart: 27, of which 8 were waited for; matrix products, arithmetic and copies ran while one was open for 10% of the time, Pallas kernels for 0%

commit v1 on v0

v1 whole, which is shorter than its diff:
```python
import functools

import jax
import jax.numpy as jnp
from jax import lax
from jax.experimental import pallas as pl
from jax.experimental.pallas import tpu as pltpu
from jax.sharding import PartitionSpec as P

norm_eps = 0.001
lane = 128
half_taps = 8
group = 8
unit = 16
bf16 = jnp.bfloat16
f32 = jnp.float32
vmem_budget = 44 << 20

row_dot = (((1,), (1,)), ((), ()))
plain_dot = (((1,), (0,)), ((), ()))
column_dot = (((0,), (0,)), ((), ()))


def in_vmem():
    return pl.BlockSpec(memory_space=pltpu.VMEM)


def in_place():
    return pl.BlockSpec(memory_space=pl.ANY)


def in_smem():
    return pl.BlockSpec(memory_space=pltpu.SMEM)


def dot(a, b, dims):
    return lax.dot_general(a, b, dims, preferred_element_type=f32)


def cols(c):
    return slice(c * lane, (c + 1) * lane)


def sigmoid(v):
    return 1.0 / (1.0 + jnp.exp(-v))


def moments(total, row, count, samples):
    out = []
    for c in range(count):
        mean = total[row + c : row + c + 1] * (1.0 / samples)
        spread = total[row + count + c : row + count + c + 1] * (1.0 / samples) - mean * mean
        out.append((mean, lax.rsqrt(spread + norm_eps)))
    return out


def start_weights(w_hbm, w_vmem, sems, pick):
    for k in range(w_vmem.shape[0]):
        pltpu.make_async_copy(pick(w_hbm, k), w_vmem.at[k], sems.at[k]).start()


def wait_weights(w_hbm, w_vmem, sems, pick, k):
    pltpu.make_async_copy(pick(w_hbm, k), w_vmem.at[k], sems.at[k]).wait()


def convolve(rows, base, planes, seg_ref, w_hbm, w_vmem, sems, pick, flip, dims, acc_ref):
    taps = w_vmem.shape[0]
    blocks = planes.shape[0]
    for k in range(taps):
        tap = taps - 1 - k if flip else k
        wait_weights(w_hbm, w_vmem, sems, pick, tap)
        mask = (
            seg_ref[base + k : base + k + rows]
            == seg_ref[base + half_taps : base + half_taps + rows]
        )
        x = jnp.concatenate(
            [jnp.where(mask, planes[c, k : k + rows], 0.0).astype(bf16) for c in range(blocks)],
            axis=1,
        )
        d = dot(x, w_vmem[tap], dims)
        if k == 0:
            acc_ref[...] = d
        else:
            acc_ref[...] += d


def broadcast_sums(snd_ref, pieces):
    tile = jnp.concatenate(pieces, axis=0)
    if tile.shape[0] < snd_ref.shape[1]:
        tile = jnp.concatenate(
            [tile, jnp.zeros((snd_ref.shape[1] - tile.shape[0], lane), f32)], axis=0
        )
    for d in range(snd_ref.shape[0]):
        snd_ref[d] = tile


def sum_rows(v):
    return jnp.sum(v, axis=0, keepdims=True)


def forward_first(frames, ext, base, pick, x_ref, seg_ref, w_ref, a_ref, snd_ref, planes, w_vmem, sems):
    start_weights(w_ref, w_vmem, sems, pick)
    for c in range(planes.shape[0]):
        planes[c] = x_ref[:, cols(c)].astype(f32)
    rows = a_ref.shape[0]
    convolve(rows, base, planes, seg_ref, w_ref, w_vmem, sems, pick, False, row_dot, a_ref)
    own = slice(ext, ext + frames)
    first, second = [], []
    for c in range(a_ref.shape[1] // lane):
        v = a_ref[own, cols(c)]
        first.append(sum_rows(v))
        second.append(sum_rows(v * v))
    broadcast_sums(snd_ref, first + second)


def forward_next(
    frames, ext, base, samples, pick,
    prev_ref, st_ref, gs_ref, seg_ref, w_ref,
    a_ref, h_ref, snd_ref,
    planes, w_vmem, sems,
):
    start_weights(w_ref, w_vmem, sems, pick)
    blocks = planes.shape[0]
    total = jnp.sum(st_ref[...], axis=0)
    inner = slice(ext + half_taps, ext + half_taps + frames)
    for c, (mean, rstd) in enumerate(moments(total, 0, blocks, samples)):
        z = (prev_ref[:, cols(c)] - mean) * (rstd * gs_ref[c : c + 1])
        z = z + gs_ref[blocks + c : blocks + c + 1]
        low = (z * sigmoid(z)).astype(bf16)
        planes[c] = low.astype(f32)
        h_ref[:, cols(c)] = low[inner]
    convolve(a_ref.shape[0], base, planes, seg_ref, w_ref, w_vmem, sems, pick, False, row_dot, a_ref)
    own = slice(ext, ext + frames)
    first, second = [], []
    for c in range(blocks):
        v = a_ref[own, cols(c)]
        first.append(sum_rows(v))
        second.append(sum_rows(v * v))
    broadcast_sums(snd_ref, first + second)


def branch_operands(pl_ref, x_ref, rw_ref, rows, offset, x_offset, branch):
    sizes = (pl_ref.shape[1] // 2, pl_ref.shape[1] // 2, x_ref.shape[1])
    at = sum(sizes[:branch])
    w = rw_ref[:, at : at + sizes[branch]]
    if branch == 2:
        return x_ref[x_offset : x_offset + rows], w
    return pl_ref[offset : offset + rows, at : at + sizes[branch]], w


def branch_sums(frames, pl_ext, x_ext, pl_ref, x_ref, rw_ref, snd_ref):
    blocks = rw_ref.shape[0] // lane
    pieces = []
    for branch in range(3):
        p, w = branch_operands(pl_ref, x_ref, rw_ref, frames, pl_ext, x_ext, branch)
        q = dot(p, w, row_dot)
        pieces += [sum_rows(q[:, cols(c)]) for c in range(blocks)]
        pieces += [sum_rows(q[:, cols(c)] * q[:, cols(c)]) for c in range(blocks)]
    broadcast_sums(snd_ref, pieces)


def join(
    frames, ext, x_ext, samples,
    a_ref, st_ref, gs_ref, pl_ref, x_ref, rw_ref, qst_ref, rgs_ref, cot_ref,
    out_ref, du_ref, snd_ref, snd_res_ref,
    q_ref,
):
    rows, blocks = a_ref.shape[0], a_ref.shape[1] // lane
    for branch in range(3):
        p, w = branch_operands(pl_ref, x_ref, rw_ref, rows, 0, x_ext - ext, branch)
        q_ref[branch] = dot(p, w, row_dot)
    total = jnp.sum(st_ref[...], axis=0)
    res_total = jnp.sum(qst_ref[...], axis=0)
    main = moments(total, 0, blocks, samples)
    res = [moments(res_total, 2 * blocks * branch, blocks, samples) for branch in range(3)]
    own = slice(ext, ext + frames)
    shift_sums, gain_sums, res_sums = [], [], [[], [], []]
    for c in range(blocks):
        normed = (a_ref[:, cols(c)] - main[c][0]) * main[c][1]
        u = normed * gs_ref[c : c + 1] + gs_ref[blocks + c : blocks + c + 1]
        for branch in range(3):
            mean, rstd = res[branch][c]
            at = branch * blocks + c
            qn = (q_ref[branch, :, cols(c)] - mean) * rstd
            q_ref[branch, :, cols(c)] = qn
            u = u + qn * rgs_ref[at : at + 1] + rgs_ref[3 * blocks + at : 3 * blocks + at + 1]
        s = sigmoid(u)
        out_ref[:, cols(c)] = (u * s)[own].astype(bf16)
        du = cot_ref[:, cols(c)].astype(f32) * (s * (1.0 + u * (1.0 - s)))
        du_ref[:, cols(c)] = du
        du = du[own]
        shift_sums.append(sum_rows(du))
        gain_sums.append(sum_rows(du * normed[own]))
        for branch in range(3):
            res_sums[branch].append(sum_rows(du * q_ref[branch, own, cols(c)]))
    broadcast_sums(snd_ref, shift_sums + gain_sums)
    broadcast_sums(snd_res_ref, res_sums[0] + res_sums[1] + res_sums[2])


def branch_grads(
    frames, ext, x_ext, samples,
    du_ref, bst_ref, rst_ref, pl_ref, x_ref, rw_ref, qst_ref, rgs_ref,
    g0_ref, g1_ref, g2_ref, gw_ref,
):
    blocks = rw_ref.shape[0] // lane
    total = jnp.sum(bst_ref[...], axis=0) * (1.0 / samples)
    gains = jnp.sum(rst_ref[...], axis=0) * (1.0 / samples)
    res_total = jnp.sum(qst_ref[...], axis=0)
    own = slice(ext, ext + frames)
    at_col = 0
    for branch, g_ref in enumerate((g0_ref, g1_ref, g2_ref)):
        p, w = branch_operands(pl_ref, x_ref, rw_ref, frames, ext, x_ext, branch)
        q = dot(p, w, row_dot)
        low = []
        for c, (mean, rstd) in enumerate(moments(res_total, 2 * blocks * branch, blocks, samples)):
            at = branch * blocks + c
            qn = (q[:, cols(c)] - mean) * rstd
            v = du_ref[own, cols(c)] - total[c : c + 1] - qn * gains[at : at + 1]
            low.append((v * (rgs_ref[at : at + 1] * rstd)).astype(bf16))
        low = jnp.concatenate(low, axis=1)
        g_ref[...] = dot(low, w, plain_dot).astype(g_ref.dtype)
        width = p.shape[1]
        gw_ref[:, at_col : at_col + width] = dot(low, p, column_dot).astype(bf16)
        at_col += width


def backward_step(
    frames, ext_da, off_a, off_prev, base, samples, pick, last,
    table_ref, dz_ref, bst_ref, a_ref, st_ref, gs_ref, seg_ref, w_ref, prev_ref, prev_st_ref, prev_gs_ref,
    out_ref, x_ref, snd_ref,
    planes, turned, w_vmem, sems, acc_ref,
):
    start_weights(w_ref, w_vmem, sems, pick)
    rows, blocks = dz_ref.shape[0], dz_ref.shape[1] // lane
    sums = jnp.sum(bst_ref[...], axis=0) * (1.0 / samples)
    total = jnp.sum(st_ref[...], axis=0)
    for c, (mean, rstd) in enumerate(moments(total, 0, blocks, samples)):
        normed = (a_ref[off_a : off_a + rows, cols(c)] - mean) * rstd
        v = dz_ref[:, cols(c)] - sums[c : c + 1] - normed * sums[blocks + c : blocks + c + 1]
        planes[c, 0:rows] = (v * (gs_ref[c : c + 1] * rstd)).astype(bf16).astype(f32)
    at = ext_da - half_taps
    wide = turned.shape[1]
    for c in range(blocks):
        turned[cols(c), :] = planes[c, at : at + wide].T.astype(bf16)
    for r in range(group):
        for s in range(4):
            row = pl.multiple_of(table_ref[4 * r + s], unit)
            x_ref[r & 1, (r >> 1) & 1, r >> 2, s * unit : (s + 1) * unit, :] = turned[
                pl.ds(row, unit), :
            ]
    out_rows = rows - 2 * half_taps
    convolve(
        out_rows, base, planes, seg_ref, w_ref, w_vmem, sems, pick, True, plain_dot, acc_ref
    )
    if last:
        out_ref[...] = (acc_ref[...] + prev_ref[...]).astype(out_ref.dtype)
        return
    prev_total = jnp.sum(prev_st_ref[...], axis=0)
    own = slice(ext_da - half_taps, ext_da - half_taps + frames)
    shift_sums, gain_sums = [], []
    for c, (mean, rstd) in enumerate(moments(prev_total, 0, blocks, samples)):
        normed = (prev_ref[off_prev : off_prev + out_rows, cols(c)] - mean) * rstd
        z = normed * prev_gs_ref[c : c + 1] + prev_gs_ref[blocks + c : blocks + c + 1]
        s = sigmoid(z)
        dz = acc_ref[:, cols(c)] * (s * (1.0 + z * (1.0 - s)))
        out_ref[:, cols(c)] = dz
        dz = dz[own]
        shift_sums.append(sum_rows(dz))
        gain_sums.append(sum_rows(dz * normed[own]))
    broadcast_sums(snd_ref, shift_sums + gain_sums)


def weight_grads(frames, taps, sources, x_refs, h_refs, segs_ref, keep_ref, send_ref, left, acc_ref, h_vmem, sems):
    chunks = len(sources)

    def copies(r):
        slot = r % 2
        at, made = 0, []
        for n, (i, index, rows) in enumerate(sources[r][1]):
            src = h_refs[i].at[index] if index is not None else h_refs[i]
            made.append(
                pltpu.make_async_copy(src, h_vmem.at[slot, at : at + rows], sems.at[slot, n])
            )
            at += rows
        return made

    for copy in copies(0):
        copy.start()
    for r in range(chunks):
        if r + 1 < chunks:
            for copy in copies(r + 1):
                copy.start()
        i, index = sources[r][0]
        part = x_refs[i][index]
        seg = segs_ref[r]
        centre = seg[:, half_taps : half_taps + frames]
        for k in range(taps):
            mask = jnp.where(seg[:, k : k + frames] == centre, 1.0, 0.0).astype(bf16)
            mask = jnp.concatenate([mask] * (4 * unit // mask.shape[0]), axis=0)
            left[(taps - 1 - k) * 4 * unit : (taps - k) * 4 * unit, :] = (
                part[:, k : k + frames] * mask
            )
        for copy in copies(r):
            copy.wait()
        d = dot(left[...], h_vmem[r % 2], plain_dot)
        if r == 0:
            acc_ref[...] = d
        else:
            acc_ref[...] += d
    for k in range(taps):
        at = k * 4 * unit
        keep_ref[k] = acc_ref[at : at + 2 * unit]
        send_ref[k] = acc_ref[at + 2 * unit : at + 4 * unit].astype(bf16)


def call(body, name, out_shape, in_specs, scratch, flops, byte_count, args, out_specs=None):
    out_specs = out_specs or jax.tree.map(lambda _: in_vmem(), out_shape)
    return pl.pallas_call(
        body,
        out_shape=out_shape,
        in_specs=in_specs,
        out_specs=out_specs,
        scratch_shapes=scratch,
        compiler_params=pltpu.CompilerParams(vmem_limit_bytes=vmem_budget),
        cost_estimate=pl.CostEstimate(flops=flops, bytes_accessed=byte_count, transcendentals=0),
        name=name,
    )(*args)


def per_device(
    block_entry_input,
    prelude_output,
    leading_block_output,
    lengths,
    leading_conv_weight,
    remaining_conv_weight,
    gain,
    shift,
    residual_pointwise_weight,
    residual_norm_scale,
    residual_norm_bias,
    cotangent,
):
    tm, rows_axis = lax.axis_size("tm"), lax.axis_size("batch")
    everyone = ("tm", "batch")
    devices = tm * rows_axis
    place = lax.axis_index("tm")
    row_place = lax.axis_index("batch")
    frames, entry_width = block_entry_input.shape[1:]
    channels, taps = leading_conv_weight.shape[:2]
    blocks = channels // lane
    layers = remaining_conv_weight.shape[0] + 1
    samples = float(frames * tm * rows_axis)
    reach = half_taps * 2 * layers
    ext = [reach - half_taps * i for i in range(layers + 1)]
    ext_u = ext[layers]
    split_rows = rows_axis == 2 and channels // tm == 2 * unit

    def sds(shape, dtype):
        return jax.ShapeDtypeStruct(shape, dtype)

    def swap(v, axis, bit):
        n = lax.axis_size(axis)
        return lax.ppermute(v, axis, [(i, i ^ bit) for i in range(n)])

    def spread(v):
        return lax.all_to_all(v, everyone, 0, 0, tiled=True)

    x_own, cot_own = block_entry_input[0], cotangent[0]
    pl_own = jnp.concatenate([prelude_output[0], leading_block_output[0]], axis=1)

    def edge(part):
        side = jnp.concatenate([part(pl_own, ext_u), part(cot_own, ext_u)], axis=0)
        return jnp.concatenate([part(x_own, reach), side], axis=1)

    tail_rows = edge(lambda v, n: v[frames - n :])
    head_rows = edge(lambda v, n: v[:n])
    low = lax.ppermute(tail_rows, "tm", [(i, i + 1) for i in range(tm - 1)])
    high = lax.ppermute(head_rows, "tm", [(i + 1, i) for i in range(tm - 1)])
    x_ext = jnp.concatenate([low[:, :entry_width], x_own, high[:, :entry_width]], axis=0)
    pl_ext = jnp.concatenate(
        [low[:ext_u, entry_width:], pl_own, high[:ext_u, entry_width:]], axis=0
    )
    cot_ext = jnp.concatenate(
        [low[ext_u:, entry_width:], cot_own, high[ext_u:, entry_width:]], axis=0
    )

    counts = lengths[0]
    number = counts.shape[0]
    order = jnp.arange(number)
    starts = jnp.sum(jnp.where(order[None, :] < order[:, None], counts[None, :], 0), axis=1)

    def segments(position):
        inside = sum((position >= starts[j]).astype(f32) for j in range(number))
        inside = jnp.where(position < 0, 0.0, inside)
        return jnp.where(position < frames * tm, inside, -1.0)

    seg = segments(
        place * frames - reach + lax.broadcasted_iota(jnp.int32, (frames + 2 * reach, lane), 0)
    )
    wide = -(-(frames + 2 * half_taps) // lane) * lane
    relative = lax.broadcasted_iota(jnp.int32, (group, unit, wide), 0)
    segs = segments(
        (place ^ relative) * frames
        - half_taps
        + lax.broadcasted_iota(jnp.int32, (group, unit, wide), 2)
    )

    peer = (jnp.arange(group, dtype=jnp.int32) ^ (place % group))[:, None]
    slot = jnp.arange(4, dtype=jnp.int32)[None, :]
    high_place = place // group
    if split_rows:
        table = ((high_place ^ (slot % 2)) * group + peer) * (2 * unit)
        table = table + (row_place ^ (slot // 2)) * unit
    else:
        table = ((high_place ^ slot) * group + peer) * unit
    table = table.reshape(-1).astype(jnp.int32)

    w_first = jnp.transpose(leading_conv_weight, (1, 0, 2))
    w_rest = jnp.transpose(remaining_conv_weight, (0, 2, 1, 3))

    def weights(layer):
        if layer == 1:
            return w_first, (lambda ref, k: ref.at[k]), entry_width
        return w_rest, (lambda ref, k, at=layer - 2: ref.at[at, k]), channels

    def gain_shift(layer):
        return jnp.concatenate([gain[layer - 1], shift[layer - 1]]).reshape(2 * blocks, lane)

    gs = [None] + [gain_shift(i) for i in range(1, layers + 1)]
    res_gs = jnp.concatenate([residual_norm_scale, residual_norm_bias]).reshape(6 * blocks, lane)
    tile_sums = sds((devices, 2 * blocks, lane), f32)
    res_rows = -(-3 * blocks // 8) * 8

    def conv_scratch(planes_rows, width, w_shape):
        return [
            pltpu.VMEM((width // lane, planes_rows, lane), f32),
            pltpu.VMEM(w_shape, bf16),
            pltpu.SemaphoreType.DMA((taps,)),
        ]

    def conv_cost(rows, width):
        return 2 * rows * width * channels * taps, 2 * taps * width * channels + 8 * rows * channels

    def gather(h):
        over_y = swap(h, "tm", 2)
        over_z = swap(h, "tm", 4)
        half = frames // 2
        corner_a = swap(over_y[:half], "tm", 4)
        corner_b = swap(over_z[half:], "tm", 2)
        mine = [h, over_y, over_z, corner_a, corner_b]
        return mine + [swap(v, "tm", 1) for v in mine]

    def h_sources():
        full = frames
        half = frames // 2
        by_pair = {0: [(0, None, full)], 1: [(1, None, full)], 2: [(2, None, full)],
                   3: [(3, None, half), (4, None, half)]}
        out = []
        for r in range(group):
            entries = by_pair[r >> 1]
            out.append(tuple((i + 5 * (r & 1), index, n) for i, index, n in entries))
        return out

    def exchange(x):
        r1 = swap(x[1], "tm", 1)
        r2 = swap(jnp.stack([x[0, 1], r1[1]]), "tm", 2)
        r3 = swap(jnp.stack([x[0, 0, 1], r1[0, 1], r2[0, 1], r2[1, 1]]), "tm", 4)
        return [x, r1, r2, r3]

    x_sources = [
        (0, (0, 0, 0)), (1, (0, 0)), (2, (0, 0)), (2, (1, 0)),
        (3, (0,)), (3, (1,)), (3, (2,)), (3, (3,)),
    ]

    def weight_gradient(layer, parts, gathered):
        width = gathered[0].shape[1]
        sources = list(zip(x_sources, h_sources(), strict=True))
        nx, nh = len(parts), len(gathered)

        def body(*refs):
            x_refs, h_refs = refs[:nx], refs[nx : nx + nh]
            weight_grads(frames, taps, sources, x_refs, h_refs, *refs[nx + nh :])

        keep, send = call(
            body, "weight_grads",
            (sds((taps, 2 * unit, width), f32), sds((taps, 2 * unit, width), bf16)),
            [in_vmem()] * nx + [in_place()] * nh + [in_vmem()],
            [
                pltpu.VMEM((taps * 4 * unit, frames), bf16),
                pltpu.VMEM((taps * 4 * unit, width), f32),
                pltpu.VMEM((2, frames, width), bf16),
                pltpu.SemaphoreType.DMA((2, 2)),
            ],
            2 * taps * 4 * unit * frames * group * width,
            2 * group * frames * width,
            (*parts, *gathered, segs),
        )
        return keep, send

    def reduce_gradient(keep, send):
        first = ("batch", 1) if split_rows else ("tm", 2 * group)
        both = keep + swap(send, *first).astype(f32)
        part = both[:, :unit] + swap(both[:, unit:].astype(bf16), "tm", group).astype(f32)
        if not split_rows:
            return lax.psum(part.astype(bf16), "batch").astype(f32)
        part = part.astype(bf16)
        other = swap(part, "batch", 1)
        top = jnp.where(row_place == 0, part, other)
        bottom = jnp.where(row_place == 0, other, part)
        return jnp.concatenate([top, bottom], axis=1).astype(f32)

    row_count = [frames + 2 * e for e in ext]
    w, pick, width = weights(1)
    rows = row_count[1]
    flops, moved = conv_cost(rows, width)
    a, snd = call(
        functools.partial(forward_first, frames, ext[1], reach - ext[0], pick), "forward_first",
        (sds((rows, channels), f32), tile_sums),
        [in_vmem(), in_vmem(), in_place()],
        conv_scratch(row_count[0], width, (taps, channels, width)),
        flops, moved, (x_ext, seg, w),
    )
    stats = [None, spread(snd)]
    acts = [None, a]
    gathered = [gather(x_own)]
    q_snd = call(
        functools.partial(branch_sums, frames, ext_u, reach), "branch_sums",
        sds((devices, 6 * blocks, lane), f32),
        [in_vmem()] * 3, [], 2 * frames * residual_pointwise_weight.size, 4 << 20,
        (pl_ext, x_ext, residual_pointwise_weight),
    )
    q_stats = spread(q_snd)
    for layer in range(2, layers + 1):
        w, pick, width = weights(layer)
        rows = row_count[layer]
        flops, moved = conv_cost(rows, width)
        a, h, snd = call(
            functools.partial(
                forward_next, frames, ext[layer], reach - ext[layer - 1], samples, pick
            ),
            "forward_next",
            (sds((rows, channels), f32), sds((frames, channels), bf16), tile_sums),
            [in_vmem()] * 4 + [in_place()],
            conv_scratch(row_count[layer - 1], width, (taps, channels, width)),
            flops, moved, (acts[-1], stats[-1], gs[layer - 1], seg, w),
        )
        stats.append(spread(snd))
        acts.append(a)
        gathered.append(gather(h))

    rows = row_count[layers]
    block_output, dz, snd, res_snd = call(
        functools.partial(join, frames, ext_u, reach, samples), "join",
        (
            sds((frames, channels), bf16), sds((rows, channels), f32), tile_sums,
            sds((devices, res_rows, lane), f32),
        ),
        [in_vmem()] * 9,
        [pltpu.VMEM((3, rows, channels), f32)],
        2 * rows * residual_pointwise_weight.size, 8 << 20,
        (
            acts[layers], stats[layers], gs[layers], pl_ext, x_ext, residual_pointwise_weight,
            q_stats, res_gs, cot_ext,
        ),
    )
    du = dz
    back = [None] * (layers + 1)
    back[layers] = spread(snd)
    res_back = spread(res_snd)

    prelude_gradient, grad_first, res_entry, res_weight = call(
        functools.partial(branch_grads, frames, ext_u, reach, samples), "branch_grads",
        (
            sds((frames, prelude_output.shape[2]), bf16),
            sds((frames, leading_block_output.shape[2]), bf16),
            sds((frames, entry_width), f32),
            sds(residual_pointwise_weight.shape, bf16),
        ),
        [in_vmem()] * 8, [], 6 * frames * residual_pointwise_weight.size, 8 << 20,
        (du, back[layers], res_back, pl_ext, x_ext, residual_pointwise_weight, q_stats, res_gs),
    )
    res_share = lax.psum_scatter(res_weight, "tm", scatter_dimension=0, tiled=True)
    if rows_axis == 2:
        grad_res_weight = res_share.astype(f32) + swap(res_share, "batch", 1).astype(f32)
    else:
        grad_res_weight = lax.psum(res_share, "batch").astype(f32)

    grads = [None] * (layers + 1)
    for layer in range(layers, 0, -1):
        w, pick, width = weights(layer)
        ext_da = half_taps * layer
        rows = frames + 2 * ext_da
        out_rows = rows - 2 * half_taps
        last = layer == 1
        flops, moved = conv_cost(out_rows, width)
        prev = (res_entry, stats[1], gs[1]) if last else (
            acts[layer - 1], stats[layer - 1], gs[layer - 1]
        )
        out = sds((out_rows, width), bf16 if last else f32)
        planes_rows = max(rows, ext_da - half_taps + wide)
        dz, x, snd = call(
            functools.partial(
                backward_step, frames, ext_da, ext[layer] - ext_da,
                ext[layer - 1] - (ext_da - half_taps), reach - ext_da, samples, pick, last,
            ),
            "backward_step",
            (out, sds((2, 2, 2, 4 * unit, wide), bf16), tile_sums),
            [in_smem()] + [in_vmem()] * 6 + [in_place()] + [in_vmem()] * 3,
            [
                pltpu.VMEM((blocks, planes_rows, lane), f32),
                pltpu.VMEM((channels, wide), bf16),
                pltpu.VMEM((taps, channels, width), bf16),
                pltpu.SemaphoreType.DMA((taps,)),
                pltpu.VMEM((out_rows, width), f32),
            ],
            flops, moved,
            (table, dz, back[layer], acts[layer], stats[layer], gs[layer], seg, w, *prev),
        )
        if not last:
            back[layer - 1] = spread(snd)
        keep, send = weight_gradient(layer, exchange(x), gathered[layer - 1])
        grads[layer] = reduce_gradient(keep, send)

    grad_block_input = dz[None]
    width_dev = channels // tm

    def share(v):
        return lax.dynamic_slice_in_dim(v, place * width_dev, width_dev, axis=v.ndim - 1)

    sums = [None] + [jnp.sum(back[i], axis=0).reshape(2, channels) for i in range(1, layers + 1)]
    grad_gain = share(jnp.stack([sums[i][1] for i in range(1, layers + 1)]))
    grad_shift = share(jnp.stack([sums[i][0] for i in range(1, layers)]))
    grad_last_shift = share(sums[layers][0])
    res_sums = jnp.sum(res_back, axis=0)[: 3 * blocks].reshape(3, channels)
    grad_res_gain = share(res_sums)
    grad_res_shift = jnp.broadcast_to(grad_last_shift[None], (3, width_dev))
    grad_w_first = jnp.transpose(grads[1], (1, 0, 2))
    grad_w_rest = jnp.transpose(jnp.stack(grads[2:]), (0, 2, 1, 3))
    return (
        block_output[None],
        grad_block_input,
        prelude_gradient[None],
        grad_first[None],
        grad_w_first,
        grad_w_rest,
        grad_gain,
        grad_shift,
        grad_last_shift,
        grad_res_weight,
        grad_res_gain,
        grad_res_shift,
    )


def solution(mesh):
    split = P("batch", "tm", None)
    in_specs = (
        split, split, split, P("batch", None), P(), P(), P(), P(), P(), P(), P(), split,
    )
    out_specs = (
        split, split, split, split,
        P("tm", None, None), P(None, "tm", None, None), P(None, "tm"), P(None, "tm"), P("tm"),
        P("tm", None), P(None, "tm"), P(None, "tm"),
    )
    return jax.shard_map(
        per_device, mesh=mesh, in_specs=in_specs, out_specs=out_specs, check_vma=False
    )
```

time: 1370 us -> 617 us (0.45)
  waiting for transfers between devices: 571 us -> 119 us
  blocking collectives: 438 us -> 0 us
  Pallas kernels: 0 us -> 195 us
  matrix products: 166 us -> 0 us
  local copies, waits for them, and re-layouts: 16.8 us -> 108 us
  starting transfers between devices: 38.1 us -> 118 us
  other arithmetic: 118 us -> 49.1 us
    reduce_scatter x5 -> x1, waiting for transfers between devices: 465 us -> 0.01 us  [per_device(): lax.psum_scatter(res_weight, 'tm', scatter_dimension=0, tiled=True)]
    psum x11 -> x0, blocking collectives: 438 us -> none  [the longest x5 208 us: per_device(): total_shift, total_gain = lax.psum((shift_sum, gain_sum), ('tm', 'batch'))]
    pallas_call x0 -> x18, Pallas kernels: none -> 195 us  [call(): pl.pallas_call(body, out_shape=out_shape, in_specs=in_specs, out_specs=ou...]
    dot_general x24 -> x0, matrix products: 166 us -> none  [the longest x5 53.7 us: per_device(): lax.dot_general(columns, weight, (((1, 2), (1, 2)), ((), ())), preferred_...]
    ppermute x20 -> x78, waiting for transfers between devices: 2.22 us -> 88.9 us  [the longest x76 88.9 us: swap(): return lax.ppermute(v, axis, [(i, i ^ bit) for i in range(n)])]
    unnamed x139 -> x0, other arithmetic: 81.1 us -> none
    psum x1 -> x0, waiting for transfers between devices: 63.2 us -> none  [per_device(): lax.psum(summed[0].astype(jnp.bfloat16), 'batch').astype(jnp.float32)]
    all_to_all x0 -> x12, starting transfers between devices: none -> 50.4 us  [spread(): return lax.all_to_all(v, everyone, 0, 0, tiled=True)]
  transfers between devices with their start and end apart: 27 -> 91, of which waited for: 8 -> 19; matrix products, arithmetic and copies ran while one was open for 10% -> 17% of each run, Pallas kernels for 0% -> 32%
where the time goes in v1:
time: 617 us; the launch traced here: 605 us
  Pallas kernels  195 us (32%)
  waiting for transfers between devices  119 us (19%)
  starting transfers between devices  118 us (19%)
  local copies, waits for them, and re-layouts  108 us (18%)
  other arithmetic  49.1 us (8%)
  between operations  15.8 us (3%)
    pallas_call x18, Pallas kernels, call(): pl.pallas_call(body, out_shape=out_shape, in_specs=in_specs, out_specs=ou...  195 us
    ppermute x76, waiting for transfers between devices, swap(): return lax.ppermute(v, axis, [(i, i ^ bit) for i in range(n)])  88.9 us
    ppermute x76, starting transfers between devices, swap(): return lax.ppermute(v, axis, [(i, i ^ bit) for i in range(n)])  63.4 us
    unnamed x230, local copies, waits for them, and re-layouts  53.3 us
    all_to_all x12, starting transfers between devices, spread(): return lax.all_to_all(v, everyone, 0, 0, tiled=True)  50.4 us
    all_to_all x12, waiting for transfers between devices, spread(): return lax.all_to_all(v, everyone, 0, 0, tiled=True)  29.8 us
  transfers between devices with their start and end apart: 91, of which 19 were waited for; matrix products, arithmetic and copies ran while one was open for 17% of the time, Pallas kernels for 32%

profile of v1, /device:TPU:0, one launch (start us, length us, event | category | flops | bytes accessed | tf_op | source)
XLA Modules:
  0.0 604.8 jit_solution(2043208672124858204)
XLA Ops:
  15.7 3.0 collective-permute-start
  19.6 10.0 %convert_add_fusion.6 = f32[672]{0:T(1024)S(1)} fusion(s32[]{:T(128)} %bitcast.23, s32[]{:T(128)} %bitcast.22, s32[]{:T(128)} %bitcast.21, s32[]{:T(128)} %bitcast.20, s32[]{:T(128)} %bitcast.19, s32[]{:T(128)} %bitcast.18, s32[]{:T(128)} %bitcast.17, s32[]{:T(128)} %bitcast.16, s32[]{:T(128)} %bitcast.15, s32[]{:T(128)} %bitcast.14, s32[]{:T(128)} %bitcast.13, ...), kind=kLoop, calls=%fused_computation.127 | loop fusion | flops 32256 | bytes 2756 | tf_op jit(solution)/shard_map/add | solution.py:394
  30.6 3.1 copy-done.72
  33.7 11.5 %forward_first.1 = (f32[656,512]{1,0:T(8,128)S(1)}, f32[32,8,128]{2,1,0:T(8,128)}) custom-call(bf16[672,384]{1,0:T(8,128)(2,1)S(1)} %pad_maximum_fusion.2.x_ref, f32[672,128]{1,0:T(8,128)S(1)} %select_select_fusion.seg_ref, bf16[17,512,384]{2,1,0:T(8,128)(2,1)S(1)} %bitcast.143), custom_call_target="tpu_custom_call" | custom-call | flops 4385144832 | bytes 9371648 | tf_op jit(solution)/shard_map/forward_first/pallas_call | solution.py:318
  45.2 4.8 all-to-all-start
  50.7 8.0 %all-to-all-done.st_ref.prev_st_ref = f32[32,8,128]{2,1,0:T(8,128)S(1)} async-done(((f32[32,8,128]{2,1,0:T(8,128)}), f32[32,8,128]{2,1,0:T(8,128)S(1)}, u32[]{:S(2)}, u32[]{:S(2)}) %all-to-all-start) | async-done | bytes 131104 | tf_op jit(solution)/shard_map/all_to_all | solution.py:367
  58.7 9.2 %forward_next.4 = (f32[640,512]{1,0:T(8,128)S(1)}, bf16[512,512]{1,0:T(8,128)(2,1)S(1)}, f32[32,8,128]{2,1,0:T(8,128)}) custom-call(f32[656,512]{1,0:T(8,128)S(1)} %get-tuple-element.58.prev_ref.a_ref, f32[32,8,128]{2,1,0:T(8,128)S(1)} %all-to-all-done.st_ref.prev_st_ref, f32[8,128]{1,0:T(8,128)S(1)} %pad_maximum_fusion.15.gs_ref.prev_gs_ref, ...), custom_call_target="tpu_custom_call" | custom-call | flops 5704253440 | bytes 11534336 | tf_op jit(solution)/shard_map/forward_next/pallas_call | solution.py:318
  71.6 8.6 %all-to-all-done.1.st_ref.prev_st_ref = f32[32,8,128]{2,1,0:T(8,128)S(1)} async-done(((f32[32,8,128]{2,1,0:T(8,128)}), f32[32,8,128]{2,1,0:T(8,128)S(1)}, u32[]{:S(2)}, u32[]{:S(2)}) %all-to-all-start.1) | async-done | bytes 131104 | tf_op jit(solution)/shard_map/all_to_all | solution.py:367
  80.1 9.1 %forward_next.5 = (f32[624,512]{1,0:T(8,128)S(1)}, bf16[512,512]{1,0:T(8,128)(2,1)S(1)}, f32[32,8,128]{2,1,0:T(8,128)}) custom-call(f32[640,512]{1,0:T(8,128)S(1)} %get-tuple-element.60.prev_ref.a_ref, f32[32,8,128]{2,1,0:T(8,128)S(1)} %all-to-all-done.1.st_ref.prev_st_ref, f32[8,128]{1,0:T(8,128)S(1)} %pad_maximum_fusion.16.gs_ref.prev_gs_ref, ...), custom_call_target="tpu_custom_call" | custom-call | flops 5561647104 | bytes 11468800 | tf_op jit(solution)/shard_map/forward_next/pallas_call | solution.py:318
  93.8 7.5 %all-to-all-done.2.st_ref.prev_st_ref = f32[32,8,128]{2,1,0:T(8,128)S(1)} async-done(((f32[32,8,128]{2,1,0:T(8,128)}), f32[32,8,128]{2,1,0:T(8,128)S(1)}, u32[]{:S(2)}, u32[]{:S(2)}) %all-to-all-start.2) | async-done | bytes 131104 | tf_op jit(solution)/shard_map/all_to_all | solution.py:367
  101.3 8.9 %forward_next.6 = (f32[608,512]{1,0:T(8,128)S(1)}, bf16[512,512]{1,0:T(8,128)(2,1)}, f32[32,8,128]{2,1,0:T(8,128)}) custom-call(f32[624,512]{1,0:T(8,128)S(1)} %get-tuple-element.62.prev_ref.a_ref, f32[32,8,128]{2,1,0:T(8,128)S(1)} %all-to-all-done.2.st_ref.prev_st_ref, f32[8,128]{1,0:T(8,128)S(1)} %pad_maximum_fusion.17.gs_ref.prev_gs_ref, ...), custom_call_target="tpu_custom_call" | custom-call | flops 5419040768 | bytes 11403264 | tf_op jit(solution)/shard_map/forward_next/pallas_call | solution.py:318
  111.2 3.3 all-to-all-start.3
  118.8 4.3 all-to-all-done.3.st_ref.prev_st_ref
  123.1 3.7 all-to-all-start.5
  131.3 9.4 %forward_next.7 = (f32[592,512]{1,0:T(8,128)S(1)}, bf16[512,512]{1,0:T(8,128)(2,1)}, f32[32,8,128]{2,1,0:T(8,128)S(1)}) custom-call(f32[608,512]{1,0:T(8,128)S(1)} %copy-done.1, f32[32,8,128]{2,1,0:T(8,128)} %all-to-all-done.3.st_ref.prev_st_ref, f32[8,128]{1,0:T(8,128)S(1)} %pad_maximum_fusion.18.gs_ref.prev_gs_ref, ...), custom_call_target="tpu_custom_call" | custom-call | flops 5276434432 | bytes 11337728 | tf_op jit(solution)/shard_map/forward_next/pallas_call | solution.py:318
  142.4 4.9 all-to-all-start.4
  163.6 3.9 join.1
  169.9 4.8 all-to-all-start.6
  176.4 11.7 %select_select_fusion.1.refs_14_ = f32[8,16,640]{2,1,0:T(8,128)} fusion(s32[]{:T(128)} %bitcast.23, s32[]{:T(128)} %bitcast.22, s32[]{:T(128)} %bitcast.21, s32[]{:T(128)} %bitcast.20, s32[]{:T(128)} %bitcast.19, s32[]{:T(128)} %bitcast.18, s32[]{:T(128)} %bitcast.17, s32[]{:T(128)} %bitcast.16, s32[]{:T(128)} %bitcast.15, s32[]{:T(128)} %bitcast.14, ...), kind=kLoop, calls=%fused_computation.40 | loop fusion | flops 4259840 | bytes 327776 | tf_op jit(solution)/shard_map/jit(_where)/select_n | solution.py:396
  204.6 4.1 all-to-all-start.11
  213.3 11.4 %backward_step.5 = (f32[576,512]{1,0:T(8,128)S(1)}, bf16[2,2,2,64,640]{4,3,2,1,0:T(8,128)(2,1)S(1)}, f32[32,8,128]{2,1,0:T(8,128)S(1)}) custom-call(s32[32]{0:T(128)S(1)} %copy-done.70, f32[592,512]{1,0:T(8,128)S(1)} %copy-done.23, f32[32,8,128]{2,1,0:T(8,128)} %all-to-all-done.6.bst_ref, f32[592,512]{1,0:T(8,128)S(1)} %copy-done.8, ...), custom_call_target="tpu_custom_call" | custom-call | flops 5133828096 | bytes 11272192 | tf_op jit(solution)/shard_map/backward_step/pallas_call | solution.py:318
  230.2 5.9 all-to-all-start.7
  248.0 3.2 branch_grads.1
  257.4 12.0 %backward_step.6 = (f32[560,512]{1,0:T(8,128)S(1)}, bf16[2,2,2,64,640]{4,3,2,1,0:T(8,128)(2,1)S(1)}, f32[32,8,128]{2,1,0:T(8,128)}) custom-call(s32[32]{0:T(128)S(1)} %copy-done.71, f32[576,512]{1,0:T(8,128)S(1)} %copy-done.28, f32[32,8,128]{2,1,0:T(8,128)} %all-to-all-done.7.bst_ref, f32[608,512]{1,0:T(8,128)S(1)} %copy-done.3, ...), custom_call_target="tpu_custom_call" | custom-call | flops 4991221760 | bytes 11206656 | tf_op jit(solution)/shard_map/backward_step/pallas_call | solution.py:318
  272.0 4.2 all-to-all-start.8
  286.1 10.7 %backward_step.7 = (f32[544,512]{1,0:T(8,128)S(1)}, bf16[2,2,2,64,640]{4,3,2,1,0:T(8,128)(2,1)S(1)}, f32[32,8,128]{2,1,0:T(8,128)S(1)}) custom-call(s32[32]{0:T(128)S(1)} %copy-done.71, f32[560,512]{1,0:T(8,128)S(1)} %copy-done.30, f32[32,8,128]{2,1,0:T(8,128)S(1)} %all-to-all-done.8.bst_ref, f32[624,512]{1,0:T(8,128)S(1)} %get-tuple-element.62.prev_ref.a_ref, ...), custom_call_target="tpu_custom_call" | custom-call | flops 4848615424 | bytes 11141120 | tf_op jit(solution)/shard_map/backward_step/pallas_call | solution.py:318
  299.4 4.3 all-to-all-start.9
  311.5 5.0 collective-permute-done.63.refs_2_
  320.2 11.4 %backward_step.8 = (f32[528,512]{1,0:T(8,128)S(1)}, bf16[2,2,2,64,640]{4,3,2,1,0:T(8,128)(2,1)S(1)}, f32[32,8,128]{2,1,0:T(8,128)}) custom-call(s32[32]{0:T(128)S(1)} %copy-done.71, f32[544,512]{1,0:T(8,128)S(1)} %copy-done.32, f32[32,8,128]{2,1,0:T(8,128)S(1)} %all-to-all-done.9.bst_ref, f32[640,512]{1,0:T(8,128)S(1)} %get-tuple-element.60.prev_ref.a_ref, ...), custom_call_target="tpu_custom_call" | custom-call | flops 4706009088 | bytes 11075584 | tf_op jit(solution)/shard_map/backward_step/pallas_call | solution.py:318
  334.1 4.9 all-to-all-start.10
  346.6 5.4 collective-permute-done.48.refs_2_
  356.3 6.3 %collective-permute-done.64.refs_3_ = bf16[4,64,640]{2,1,0:T(8,128)(2,1)S(1)} collective-permute-done((bf16[4,64,640]{2,1,0:T(8,128)(2,1)S(1)}, bf16[4,64,640]{2,1,0:T(8,128)(2,1)S(1)}, u32[]{:S(2)}, u32[]{:S(2)}) %collective-permute-start.64) | collective-permute-done | bytes 327712 | tf_op jit(solution)/shard_map/ppermute | solution.py:364
  362.6 16.2 %weight_grads.9 = (f32[17,32,512]{2,1,0:T(8,128)S(1)}, bf16[17,32,512]{2,1,0:T(8,128)(2,1)S(1)}) custom-call(bf16[2,2,2,64,640]{4,3,2,1,0:T(8,128)(2,1)S(1)} %copy-done.47, bf16[2,2,64,640]{3,2,1,0:T(8,128)(2,1)} %collective-permute-done.62.refs_1_, bf16[2,2,64,640]{3,2,1,0:T(8,128)(2,1)S(1)} %copy-done.65, ...), custom_call_target="tpu_custom_call" | custom-call | flops 4563402752 | bytes 4194304 | tf_op jit(solution)/shard_map/weight_grads/pallas_call | solution.py:318
  383.0 12.0 %backward_step.9 = (bf16[512,384]{1,0:T(8,128)(2,1)}, bf16[2,2,2,64,640]{4,3,2,1,0:T(8,128)(2,1)S(1)}, f32[32,8,128]{2,1,0:T(8,128)}) custom-call(s32[32]{0:T(128)S(1)} %copy-done.71, f32[528,512]{1,0:T(8,128)S(1)} %copy-done.74, f32[32,8,128]{2,1,0:T(8,128)S(1)} %all-to-all-done.10.bst_ref, f32[656,512]{1,0:T(8,128)S(1)} %copy-done.5, ...), custom_call_target="tpu_custom_call" | custom-call | flops 3422552064 | bytes 8781824 | tf_op jit(solution)/shard_map/backward_step/pallas_call | solution.py:318
  405.2 5.8 collective-permute-done.33.refs_2_
  414.7 6.9 %collective-permute-done.49.refs_3_ = bf16[4,64,640]{2,1,0:T(8,128)(2,1)S(1)} collective-permute-done((bf16[4,64,640]{2,1,0:T(8,128)(2,1)S(1)}, bf16[4,64,640]{2,1,0:T(8,128)(2,1)S(1)}, u32[]{:S(2)}, u32[]{:S(2)}) %collective-permute-start.49) | collective-permute-done | bytes 327712 | tf_op jit(solution)/shard_map/ppermute | solution.py:364
  421.6 16.3 %weight_grads.8 = (f32[17,32,512]{2,1,0:T(8,128)S(1)}, bf16[17,32,512]{2,1,0:T(8,128)(2,1)S(1)}) custom-call(bf16[2,2,2,64,640]{4,3,2,1,0:T(8,128)(2,1)S(1)} %copy-done.45, bf16[2,2,64,640]{3,2,1,0:T(8,128)(2,1)} %collective-permute-done.47.refs_1_, bf16[2,2,64,640]{3,2,1,0:T(8,128)(2,1)S(1)} %copy-done.59, ...), custom_call_target="tpu_custom_call" | custom-call | flops 4563402752 | bytes 4194304 | tf_op jit(solution)/shard_map/weight_grads/pallas_call | solution.py:318
  443.4 5.6 collective-permute-done.18.refs_2_
  453.4 6.2 %collective-permute-done.34.refs_3_ = bf16[4,64,640]{2,1,0:T(8,128)(2,1)S(1)} collective-permute-done((bf16[4,64,640]{2,1,0:T(8,128)(2,1)S(1)}, bf16[4,64,640]{2,1,0:T(8,128)(2,1)S(1)}, u32[]{:S(2)}, u32[]{:S(2)}) %collective-permute-start.34) | collective-permute-done | bytes 327712 | tf_op jit(solution)/shard_map/ppermute | solution.py:364
  461.1 16.8 %weight_grads.7 = (f32[17,32,512]{2,1,0:T(8,128)S(1)}, bf16[17,32,512]{2,1,0:T(8,128)(2,1)S(1)}) custom-call(bf16[2,2,2,64,640]{4,3,2,1,0:T(8,128)(2,1)S(1)} %copy-done.43, bf16[2,2,64,640]{3,2,1,0:T(8,128)(2,1)} %collective-permute-done.32.refs_1_, bf16[2,2,64,640]{3,2,1,0:T(8,128)(2,1)S(1)} %collective-permute-done.33.refs_2_, ...), custom_call_target="tpu_custom_call" | custom-call | flops 4563402752 | bytes 4194304 | tf_op jit(solution)/shard_map/weight_grads/pallas_call | solution.py:318
  498.5 15.3 %weight_grads.6 = (f32[17,32,512]{2,1,0:T(8,128)S(1)}, bf16[17,32,512]{2,1,0:T(8,128)(2,1)S(1)}) custom-call(bf16[2,2,2,64,640]{4,3,2,1,0:T(8,128)(2,1)S(1)} %copy-done.39, bf16[2,2,64,640]{3,2,1,0:T(8,128)(2,1)} %collective-permute-done.17.refs_1_, bf16[2,2,64,640]{3,2,1,0:T(8,128)(2,1)S(1)} %copy-done.63, ...), custom_call_target="tpu_custom_call" | custom-call | flops 4563402752 | bytes 4194304 | tf_op jit(solution)/shard_map/weight_grads/pallas_call | solution.py:318
  518.7 11.3 %collective-permute-done.75 = bf16[17,16,512]{2,1,0:T(8,128)(2,1)S(1)} collective-permute-done((bf16[17,16,512]{2,1,0:T(8,128)(2,1)S(1)}, bf16[17,16,512]{2,1,0:T(8,128)(2,1)S(1)}, u32[]{:S(2)}, u32[]{:S(2)}) %collective-permute-start.75) | collective-permute-done | bytes 278560 | tf_op jit(solution)/shard_map/ppermute | solution.py:364
  533.1 17.5 %weight_grads.5 = (f32[17,32,384]{2,1,0:T(8,128)S(1)}, bf16[17,32,384]{2,1,0:T(8,128)(2,1)S(1)}) custom-call(bf16[2,2,2,64,640]{4,3,2,1,0:T(8,128)(2,1)S(1)} %copy-done.41, bf16[2,2,64,640]{3,2,1,0:T(8,128)(2,1)S(1)} %copy-done.53, bf16[2,2,64,640]{3,2,1,0:T(8,128)(2,1)S(1)} %copy-done.61, bf16[4,64,640]{2,1,0:T(8,128)(2,1)S(1)} %collective-permute-done.4.refs_3_, ...), custom_call_target="tpu_custom_call" | custom-call | flops 3422552064 | bytes 3145728 | tf_op jit(solution)/shard_map/weight_grads/pallas_call | solution.py:318
  555.9 7.6 %collective-permute-done.76 = bf16[17,16,512]{2,1,0:T(8,128)(2,1)S(1)} collective-permute-done((bf16[17,16,512]{2,1,0:T(8,128)(2,1)S(1)}, bf16[17,16,512]{2,1,0:T(8,128)(2,1)S(1)}, u32[]{:S(2)}, u32[]{:S(2)}) %collective-permute-start.76) | collective-permute-done | bytes 278560 | tf_op jit(solution)/shard_map/ppermute | solution.py:364
  563.9 9.7 %collective-permute-done.45 = bf16[17,16,512]{2,1,0:T(8,128)(2,1)S(1)} collective-permute-done((bf16[17,16,512]{2,1,0:T(8,128)(2,1)S(1)}, bf16[17,16,512]{2,1,0:T(8,128)(2,1)S(1)}, u32[]{:S(2)}, u32[]{:S(2)}) %collective-permute-start.45) | collective-permute-done | bytes 278560 | tf_op jit(solution)/shard_map/ppermute | solution.py:364
  574.4 4.0 collective-permute-done.61
  579.6 8.2 %collective-permute-done.15 = bf16[17,16,384]{2,1,0:T(8,128)(2,1)S(1)} collective-permute-done((bf16[17,16,384]{2,1,0:T(8,128)(2,1)S(1)}, bf16[17,16,384]{2,1,0:T(8,128)(2,1)S(1)}, u32[]{:S(2)}, u32[]{:S(2)}) %collective-permute-start.15) | collective-permute-done | bytes 208928 | tf_op jit(solution)/shard_map/ppermute | solution.py:364
  588.6 5.1 collective-permute-done.16
  (504 shorter events, 206.2 us)
Async XLA Ops:
  7.2 144.6 %collective-permute-start.5 = (bf16[512,384]{1,0:T(8,128)(2,1)}, bf16[512,384]{1,0:T(8,128)(2,1)}, u32[]{:S(2)}, u32[]{:S(2)}) collective-permute-start(bf16[512,384]{1,0:T(8,128)(2,1)} %bitcast.137), channel_id=1, source_target_pairs={{0,4},{2,6},{4,0},{6,2},{8,12},{10,14},{12,8},{14,10},{16,20},{18,... | collective-permute-start | bytes 1179656 | tf_op jit(solution)/shard_map/ppermute | solution.py:364
  10.2 142.1 %collective-permute-start.6 = (bf16[512,384]{1,0:T(8,128)(2,1)}, bf16[512,384]{1,0:T(8,128)(2,1)}, u32[]{:S(2)}, u32[]{:S(2)}) collective-permute-start(bf16[512,384]{1,0:T(8,128)(2,1)} %bitcast.138), channel_id=1, source_target_pairs={{0,8},{2,10},{4,12},{6,14},{8,0},{10,2},{12,4},{14,6},{16,24},{18,... | collective-permute-start | bytes 1179656 | tf_op jit(solution)/shard_map/ppermute | solution.py:364
  128.2 24.5 %collective-permute-start.20 = (bf16[512,512]{1,0:T(8,128)(2,1)}, bf16[512,512]{1,0:T(8,128)(2,1)}, u32[]{:S(2)}, u32[]{:S(2)}) collective-permute-start(bf16[512,512]{1,0:T(8,128)(2,1)} %copy-done.80), channel_id=1, source_target_pairs={{0,4},{2,6},{4,0},{6,2},{8,12},{10,14},{12,8},{14,10},{16,20},{18,... | collective-permute-start | bytes 1572872 | tf_op jit(solution)/shard_map/ppermute | solution.py:364
  148.6 44.5 %collective-permute-start.21 = (bf16[512,512]{1,0:T(8,128)(2,1)}, bf16[512,512]{1,0:T(8,128)(2,1)}, u32[]{:S(2)}, u32[]{:S(2)}) collective-permute-start(bf16[512,512]{1,0:T(8,128)(2,1)} %copy-done.80), channel_id=1, source_target_pairs={{0,8},{2,10},{4,12},{6,14},{8,0},{10,2},{12,4},{14,6},{16,24},{18,... | collective-permute-start | bytes 1572872 | tf_op jit(solution)/shard_map/ppermute | solution.py:364
  150.3 46.1 %collective-permute-start.35 = (bf16[512,512]{1,0:T(8,128)(2,1)}, bf16[512,512]{1,0:T(8,128)(2,1)}, u32[]{:S(2)}, u32[]{:S(2)}) collective-permute-start(bf16[512,512]{1,0:T(8,128)(2,1)} %copy-done.83), channel_id=1, source_target_pairs={{0,4},{2,6},{4,0},{6,2},{8,12},{10,14},{12,8},{14,10},{16,20},{18,... | collective-permute-start | bytes 1572872 | tf_op jit(solution)/shard_map/ppermute | solution.py:364
  151.8 47.8 %collective-permute-start.36 = (bf16[512,512]{1,0:T(8,128)(2,1)}, bf16[512,512]{1,0:T(8,128)(2,1)}, u32[]{:S(2)}, u32[]{:S(2)}) collective-permute-start(bf16[512,512]{1,0:T(8,128)(2,1)} %copy-done.83), channel_id=1, source_target_pairs={{0,8},{2,10},{4,12},{6,14},{8,0},{10,2},{12,4},{14,6},{16,24},{18,... | collective-permute-start | bytes 1572872 | tf_op jit(solution)/shard_map/ppermute | solution.py:364
  152.3 48.9 %collective-permute-start.50 = (bf16[512,512]{1,0:T(8,128)(2,1)}, bf16[512,512]{1,0:T(8,128)(2,1)}, u32[]{:S(2)}, u32[]{:S(2)}) collective-permute-start(bf16[512,512]{1,0:T(8,128)(2,1)} %get-tuple-element.96.refs_4_), channel_id=1, source_target_pairs={{0,4},{2,6},{4,0},{6,2},{8,12},{10,14},{12,8},{14,10},{16,20},{18,... | collective-permute-start | bytes 1572872 | tf_op jit(solution)/shard_map/ppermute | solution.py:364
  152.7 50.3 %collective-permute-start.51 = (bf16[512,512]{1,0:T(8,128)(2,1)}, bf16[512,512]{1,0:T(8,128)(2,1)}, u32[]{:S(2)}, u32[]{:S(2)}) collective-permute-start(bf16[512,512]{1,0:T(8,128)(2,1)} %get-tuple-element.96.refs_4_), channel_id=1, source_target_pairs={{0,8},{2,10},{4,12},{6,14},{8,0},{10,2},{12,4},{14,6},{16,24},{18,... | collective-permute-start | bytes 1572872 | tf_op jit(solution)/shard_map/ppermute | solution.py:364
  169.9 34.8 %all-to-all-start.6 = ((f32[32,8,128]{2,1,0:T(8,128)}), f32[32,8,128]{2,1,0:T(8,128)}, u32[]{:S(2)}, u32[]{:S(2)}) async-start(f32[32,8,128]{2,1,0:T(8,128)} %copy-done.54), calls=%async_computation.6 | async-start | bytes 262144 | tf_op jit(solution)/shard_map/all_to_all | solution.py:367
  194.7 42.5 %collective-permute-start.65 = (bf16[512,512]{1,0:T(8,128)(2,1)}, bf16[512,512]{1,0:T(8,128)(2,1)}, u32[]{:S(2)}, u32[]{:S(2)}) collective-permute-start(bf16[512,512]{1,0:T(8,128)(2,1)} %get-tuple-element.100.refs_4_), channel_id=1, source_target_pairs={{0,4},{2,6},{4,0},{6,2},{8,12},{10,14},{12,8},{14,10},{16,20},{18,... | collective-permute-start | bytes 1572872 | tf_op jit(solution)/shard_map/ppermute | solution.py:364
  196.4 44.2 %collective-permute-start.66 = (bf16[512,512]{1,0:T(8,128)(2,1)}, bf16[512,512]{1,0:T(8,128)(2,1)}, u32[]{:S(2)}, u32[]{:S(2)}) collective-permute-start(bf16[512,512]{1,0:T(8,128)(2,1)} %get-tuple-element.100.refs_4_), channel_id=1, source_target_pairs={{0,8},{2,10},{4,12},{6,14},{8,0},{10,2},{12,4},{14,6},{16,24},{18,... | collective-permute-start | bytes 1572872 | tf_op jit(solution)/shard_map/ppermute | solution.py:364
  199.6 141.3 %collective-permute-start.69 = (bf16[512,512]{1,0:T(8,128)(2,1)}, bf16[512,512]{1,0:T(8,128)(2,1)}, u32[]{:S(2)}, u32[]{:S(2)}) collective-permute-start(bf16[512,512]{1,0:T(8,128)(2,1)} %get-tuple-element.100.refs_4_), channel_id=1, source_target_pairs={{0,2},{2,0},{4,6},{6,4},{8,10},{10,8},{12,14},{14,12},{16,18},{18,... | collective-permute-start | bytes 1572872 | tf_op jit(solution)/shard_map/ppermute | solution.py:364
  204.6 25.6 %all-to-all-start.11 = ((f32[32,16,128]{2,1,0:T(8,128)}), f32[32,16,128]{2,1,0:T(8,128)}, u32[]{:S(2)}, u32[]{:S(2)}) async-start(f32[32,16,128]{2,1,0:T(8,128)} %copy-done.51), calls=%async_computation.11 | async-start | bytes 524288 | tf_op jit(solution)/shard_map/all_to_all | solution.py:367
  227.3 51.6 %collective-permute-start.62 = (bf16[2,2,64,640]{3,2,1,0:T(8,128)(2,1)}, bf16[2,2,64,640]{3,2,1,0:T(8,128)(2,1)}, u32[]{:S(2)}, u32[]{:S(2)}) collective-permute-start(bf16[2,2,64,640]{3,2,1,0:T(8,128)(2,1)} %slice_bitcast_fusion), channel_id=1, source_target_pairs={{0,2},{2,0},{4,6},{6,4},{8,10},{10,8},{12,14},{14,12},{16,18},{18,... | collective-permute-start | bytes 983048 | tf_op jit(solution)/shard_map/ppermute | solution.py:364
  230.2 24.6 %all-to-all-start.7 = ((f32[32,8,128]{2,1,0:T(8,128)}), f32[32,8,128]{2,1,0:T(8,128)}, u32[]{:S(2)}, u32[]{:S(2)}) async-start(f32[32,8,128]{2,1,0:T(8,128)} %copy-done.55), calls=%async_computation.7 | async-start | bytes 262144 | tf_op jit(solution)/shard_map/all_to_all | solution.py:367
  236.1 248.4 %reduce-scatter.2.cloned.1.call-start = ((), (), s32[]{:S(2)}) async-start(), calls=%async_computation.13 | async-start | bytes 974848 | tf_op jit(solution)/shard_map/reduce_scatter | solution.py:583
  239.0 107.1 %collective-permute-start.67 = (bf16[256,512]{1,0:T(8,128)(2,1)}, bf16[256,512]{1,0:T(8,128)(2,1)}, u32[]{:S(2)}, u32[]{:S(2)}) collective-permute-start(bf16[256,512]{1,0:T(8,128)(2,1)} %slice.532), channel_id=1, source_target_pairs={{0,8},{2,10},{4,12},{6,14},{8,0},{10,2},{12,4},{14,6},{16,24},{18,... | collective-permute-start | bytes 786440 | tf_op jit(solution)/shard_map/ppermute | solution.py:364
  242.3 103.8 %collective-permute-start.68 = (bf16[256,512]{1,0:T(8,128)(2,1)}, bf16[256,512]{1,0:T(8,128)(2,1)}, u32[]{:S(2)}, u32[]{:S(2)}) collective-permute-start(bf16[256,512]{1,0:T(8,128)(2,1)} %slice.533), channel_id=1, source_target_pairs={{0,4},{2,6},{4,0},{6,2},{8,12},{10,14},{12,8},{14,10},{16,20},{18,... | collective-permute-start | bytes 786440 | tf_op jit(solution)/shard_map/ppermute | solution.py:364
  243.8 111.1 %collective-permute-start.70 = (bf16[512,512]{1,0:T(8,128)(2,1)}, bf16[512,512]{1,0:T(8,128)(2,1)}, u32[]{:S(2)}, u32[]{:S(2)}) collective-permute-start(bf16[512,512]{1,0:T(8,128)(2,1)} %collective-permute-done.65.refs_5_), channel_id=1, source_target_pairs={{0,2},{2,0},{4,6},{6,4},{8,10},{10,8},{12,14},{14,12},{16,18},{18,... | collective-permute-start | bytes 1572872 | tf_op jit(solution)/shard_map/ppermute | solution.py:364
  278.9 26.6 %collective-permute-start.47 = (bf16[2,2,64,640]{3,2,1,0:T(8,128)(2,1)}, bf16[2,2,64,640]{3,2,1,0:T(8,128)(2,1)}, u32[]{:S(2)}, u32[]{:S(2)}) collective-permute-start(bf16[2,2,64,640]{3,2,1,0:T(8,128)(2,1)} %slice_bitcast_fusion.1), channel_id=1, source_target_pairs={{0,2},{2,0},{4,6},{6,4},{8,10},{10,8},{12,14},{14,12},{16,18},{18,... | collective-permute-start | bytes 983048 | tf_op jit(solution)/shard_map/ppermute | solution.py:364
  316.5 24.7 %collective-permute-start.32 = (bf16[2,2,64,640]{3,2,1,0:T(8,128)(2,1)}, bf16[2,2,64,640]{3,2,1,0:T(8,128)(2,1)}, u32[]{:S(2)}, u32[]{:S(2)}) collective-permute-start(bf16[2,2,64,640]{3,2,1,0:T(8,128)(2,1)} %slice_bitcast_fusion.2), channel_id=1, source_target_pairs={{0,2},{2,0},{4,6},{6,4},{8,10},{10,8},{12,14},{14,12},{16,18},{18,... | collective-permute-start | bytes 983048 | tf_op jit(solution)/shard_map/ppermute | solution.py:364
  334.1 46.5 %all-to-all-start.10 = ((f32[32,8,128]{2,1,0:T(8,128)}), f32[32,8,128]{2,1,0:T(8,128)S(1)}, u32[]{:S(2)}, u32[]{:S(2)}) async-start(f32[32,8,128]{2,1,0:T(8,128)} %get-tuple-element.78), calls=%async_computation.10 | async-start | bytes 262144 | tf_op jit(solution)/shard_map/all_to_all | solution.py:367
  354.3 46.4 %collective-permute-start.54 = (bf16[512,512]{1,0:T(8,128)(2,1)}, bf16[512,512]{1,0:T(8,128)(2,1)}, u32[]{:S(2)}, u32[]{:S(2)}) collective-permute-start(bf16[512,512]{1,0:T(8,128)(2,1)} %get-tuple-element.96.refs_4_), channel_id=1, source_target_pairs={{0,2},{2,0},{4,6},{6,4},{8,10},{10,8},{12,14},{14,12},{16,18},{18,... | collective-permute-start | bytes 1572872 | tf_op jit(solution)/shard_map/ppermute | solution.py:364
  354.3 50.1 %collective-permute-start.52 = (bf16[256,512]{1,0:T(8,128)(2,1)}, bf16[256,512]{1,0:T(8,128)(2,1)}, u32[]{:S(2)}, u32[]{:S(2)}) collective-permute-start(bf16[256,512]{1,0:T(8,128)(2,1)} %slice.524), channel_id=1, source_target_pairs={{0,8},{2,10},{4,12},{6,14},{8,0},{10,2},{12,4},{14,6},{16,24},{18,... | collective-permute-start | bytes 786440 | tf_op jit(solution)/shard_map/ppermute | solution.py:364
  354.9 49.7 %collective-permute-start.53 = (bf16[256,512]{1,0:T(8,128)(2,1)}, bf16[256,512]{1,0:T(8,128)(2,1)}, u32[]{:S(2)}, u32[]{:S(2)}) collective-permute-start(bf16[256,512]{1,0:T(8,128)(2,1)} %slice.525), channel_id=1, source_target_pairs={{0,4},{2,6},{4,0},{6,2},{8,12},{10,14},{12,8},{14,10},{16,20},{18,... | collective-permute-start | bytes 786440 | tf_op jit(solution)/shard_map/ppermute | solution.py:364
  356.3 56.9 %collective-permute-start.55 = (bf16[512,512]{1,0:T(8,128)(2,1)}, bf16[512,512]{1,0:T(8,128)(2,1)}, u32[]{:S(2)}, u32[]{:S(2)}) collective-permute-start(bf16[512,512]{1,0:T(8,128)(2,1)} %collective-permute-done.50.refs_5_), channel_id=1, source_target_pairs={{0,2},{2,0},{4,6},{6,4},{8,10},{10,8},{12,14},{14,12},{16,18},{18,... | collective-permute-start | bytes 1572872 | tf_op jit(solution)/shard_map/ppermute | solution.py:364
  362.6 38.6 %collective-permute-start.17 = (bf16[2,2,64,640]{3,2,1,0:T(8,128)(2,1)}, bf16[2,2,64,640]{3,2,1,0:T(8,128)(2,1)}, u32[]{:S(2)}, u32[]{:S(2)}) collective-permute-start(bf16[2,2,64,640]{3,2,1,0:T(8,128)(2,1)} %slice_bitcast_fusion.3), channel_id=1, source_target_pairs={{0,2},{2,0},{4,6},{6,4},{8,10},{10,8},{12,14},{14,12},{16,18},{18,... | collective-permute-start | bytes 983048 | tf_op jit(solution)/shard_map/ppermute | solution.py:364
  412.4 26.3 %collective-permute-start.39 = (bf16[512,512]{1,0:T(8,128)(2,1)S(1)}, bf16[512,512]{1,0:T(8,128)(2,1)S(1)}, u32[]{:S(2)}, u32[]{:S(2)}) collective-permute-start(bf16[512,512]{1,0:T(8,128)(2,1)S(1)} %copy-done.84), channel_id=1, source_target_pairs={{0,2},{2,0},{4,6},{6,4},{8,10},{10,8},{12,14},{14,12},{16,18},{18,... | collective-permute-start | bytes 1572872 | tf_op jit(solution)/shard_map/ppermute | solution.py:364
  412.6 28.8 %collective-permute-start.37 = (bf16[256,512]{1,0:T(8,128)(2,1)S(1)}, bf16[256,512]{1,0:T(8,128)(2,1)S(1)}, u32[]{:S(2)}, u32[]{:S(2)}) collective-permute-start(bf16[256,512]{1,0:T(8,128)(2,1)S(1)} %copy-done.108), channel_id=1, source_target_pairs={{0,8},{2,10},{4,12},{6,14},{8,0},{10,2},{12,4},{14,6},{16,24},{18,... | collective-permute-start | bytes 786440 | tf_op jit(solution)/shard_map/ppermute | solution.py:364
  413.3 28.2 %collective-permute-start.38 = (bf16[256,512]{1,0:T(8,128)(2,1)S(1)}, bf16[256,512]{1,0:T(8,128)(2,1)S(1)}, u32[]{:S(2)}, u32[]{:S(2)}) collective-permute-start(bf16[256,512]{1,0:T(8,128)(2,1)S(1)} %copy-done.109), channel_id=1, source_target_pairs={{0,4},{2,6},{4,0},{6,2},{8,12},{10,14},{12,8},{14,10},{16,20},{18,... | collective-permute-start | bytes 786440 | tf_op jit(solution)/shard_map/ppermute | solution.py:364
  414.6 27.3 %collective-permute-start.40 = (bf16[512,512]{1,0:T(8,128)(2,1)}, bf16[512,512]{1,0:T(8,128)(2,1)S(1)}, u32[]{:S(2)}, u32[]{:S(2)}) collective-permute-start(bf16[512,512]{1,0:T(8,128)(2,1)} %collective-permute-done.35.refs_5_), channel_id=1, source_target_pairs={{0,2},{2,0},{4,6},{6,4},{8,10},{10,8},{12,14},{14,12},{16,18},{18,... | collective-permute-start | bytes 1572872 | tf_op jit(solution)/shard_map/ppermute | solution.py:364
  442.0 35.9 %collective-permute-start.74 = (bf16[17,32,512]{2,1,0:T(8,128)(2,1)S(1)}, bf16[17,32,512]{2,1,0:T(8,128)(2,1)S(1)}, u32[]{:S(2)}, u32[]{:S(2)}) collective-permute-start(bf16[17,32,512]{2,1,0:T(8,128)(2,1)S(1)} %copy-done.76), channel_id=1, source_target_pairs={{0,1},{1,0},{2,3},{3,2},{4,5},{5,4},{6,7},{7,6},{8,9},{9,8},{10,11... | collective-permute-start | bytes 1671176 | tf_op jit(solution)/shard_map/ppermute | solution.py:364
  451.3 30.2 %collective-permute-start.24 = (bf16[512,512]{1,0:T(8,128)(2,1)S(1)}, bf16[512,512]{1,0:T(8,128)(2,1)S(1)}, u32[]{:S(2)}, u32[]{:S(2)}) collective-permute-start(bf16[512,512]{1,0:T(8,128)(2,1)S(1)} %copy-done.81), channel_id=1, source_target_pairs={{0,2},{2,0},{4,6},{6,4},{8,10},{10,8},{12,14},{14,12},{16,18},{18,... | collective-permute-start | bytes 1572872 | tf_op jit(solution)/shard_map/ppermute | solution.py:364
  451.4 28.1 %collective-permute-start.22 = (bf16[256,512]{1,0:T(8,128)(2,1)S(1)}, bf16[256,512]{1,0:T(8,128)(2,1)}, u32[]{:S(2)}, u32[]{:S(2)}) collective-permute-start(bf16[256,512]{1,0:T(8,128)(2,1)S(1)} %copy-done.107), channel_id=1, source_target_pairs={{0,8},{2,10},{4,12},{6,14},{8,0},{10,2},{12,4},{14,6},{16,24},{18,... | collective-permute-start | bytes 786440 | tf_op jit(solution)/shard_map/ppermute | solution.py:364
  452.0 27.5 %collective-permute-start.23 = (bf16[256,512]{1,0:T(8,128)(2,1)S(1)}, bf16[256,512]{1,0:T(8,128)(2,1)}, u32[]{:S(2)}, u32[]{:S(2)}) collective-permute-start(bf16[256,512]{1,0:T(8,128)(2,1)S(1)} %copy-done.106), channel_id=1, source_target_pairs={{0,4},{2,6},{4,0},{6,2},{8,12},{10,14},{12,8},{14,10},{16,20},{18,... | collective-permute-start | bytes 786440 | tf_op jit(solution)/shard_map/ppermute | solution.py:364
  459.7 20.3 %collective-permute-start.3 = (bf16[2,2,64,640]{3,2,1,0:T(8,128)(2,1)S(1)}, bf16[2,2,64,640]{3,2,1,0:T(8,128)(2,1)S(1)}, u32[]{:S(2)}, u32[]{:S(2)}) collective-permute-start(bf16[2,2,64,640]{3,2,1,0:T(8,128)(2,1)S(1)} %pad_maximum_fusion.3), channel_id=1, source_target_pairs={{0,4},{2,6},{4,0},{6,2},{8,12},{10,14},{12,8},{14,10},{16,20},{18,... | collective-permute-start | bytes 983048 | tf_op jit(solution)/shard_map/ppermute | solution.py:364
  488.8 27.6 %collective-permute-start.59 = (bf16[17,32,512]{2,1,0:T(8,128)(2,1)}, bf16[17,32,512]{2,1,0:T(8,128)(2,1)S(1)}, u32[]{:S(2)}, u32[]{:S(2)}) collective-permute-start(bf16[17,32,512]{2,1,0:T(8,128)(2,1)} %copy-done.77), channel_id=1, source_target_pairs={{0,1},{1,0},{2,3},{3,2},{4,5},{5,4},{6,7},{7,6},{8,9},{9,8},{10,11... | collective-permute-start | bytes 1671176 | tf_op jit(solution)/shard_map/ppermute | solution.py:364
  491.8 22.0 %collective-permute-start.9 = (bf16[512,384]{1,0:T(8,128)(2,1)S(1)}, bf16[512,384]{1,0:T(8,128)(2,1)S(1)}, u32[]{:S(2)}, u32[]{:S(2)}) collective-permute-start(bf16[512,384]{1,0:T(8,128)(2,1)S(1)} %bitcast.140), channel_id=1, source_target_pairs={{0,2},{2,0},{4,6},{6,4},{8,10},{10,8},{12,14},{14,12},{16,18},{18,... | collective-permute-start | bytes 1179656 | tf_op jit(solution)/shard_map/ppermute | solution.py:364
  491.8 22.6 %collective-permute-start.7 = (bf16[256,384]{1,0:T(8,128)(2,1)}, bf16[256,384]{1,0:T(8,128)(2,1)S(1)}, u32[]{:S(2)}, u32[]{:S(2)}) collective-permute-start(bf16[256,384]{1,0:T(8,128)(2,1)} %slice.500), channel_id=1, source_target_pairs={{0,8},{2,10},{4,12},{6,14},{8,0},{10,2},{12,4},{14,6},{16,24},{18,... | collective-permute-start | bytes 589832 | tf_op jit(solution)/shard_map/ppermute | solution.py:364
  492.6 25.5 %collective-permute-start.8 = (bf16[256,384]{1,0:T(8,128)(2,1)}, bf16[256,384]{1,0:T(8,128)(2,1)S(1)}, u32[]{:S(2)}, u32[]{:S(2)}) collective-permute-start(bf16[256,384]{1,0:T(8,128)(2,1)} %slice.501), channel_id=1, source_target_pairs={{0,4},{2,6},{4,0},{6,2},{8,12},{10,14},{12,8},{14,10},{16,20},{18,... | collective-permute-start | bytes 589832 | tf_op jit(solution)/shard_map/ppermute | solution.py:364
  493.4 24.8 %collective-permute-start.10 = (bf16[512,384]{1,0:T(8,128)(2,1)}, bf16[512,384]{1,0:T(8,128)(2,1)S(1)}, u32[]{:S(2)}, u32[]{:S(2)}) collective-permute-start(bf16[512,384]{1,0:T(8,128)(2,1)} %collective-permute-done.5.refs_5_), channel_id=1, source_target_pairs={{0,2},{2,0},{4,6},{6,4},{8,10},{10,8},{12,14},{14,12},{16,18},{18,... | collective-permute-start | bytes 1179656 | tf_op jit(solution)/shard_map/ppermute | solution.py:364
  530.0 21.9 %collective-permute-start.44 = (bf16[17,32,512]{2,1,0:T(8,128)(2,1)S(1)}, bf16[17,32,512]{2,1,0:T(8,128)(2,1)S(1)}, u32[]{:S(2)}, u32[]{:S(2)}) collective-permute-start(bf16[17,32,512]{2,1,0:T(8,128)(2,1)S(1)} %copy-done.79), channel_id=1, source_target_pairs={{0,1},{1,0},{2,3},{3,2},{4,5},{5,4},{6,7},{7,6},{8,9},{9,8},{10,11... | collective-permute-start | bytes 1671176 | tf_op jit(solution)/shard_map/ppermute | solution.py:364
  530.9 32.7 %collective-permute-start.29 = (bf16[17,32,512]{2,1,0:T(8,128)(2,1)S(1)}, bf16[17,32,512]{2,1,0:T(8,128)(2,1)S(1)}, u32[]{:S(2)}, u32[]{:S(2)}) collective-permute-start(bf16[17,32,512]{2,1,0:T(8,128)(2,1)S(1)} %get-tuple-element.90), channel_id=1, source_target_pairs={{0,1},{1,0},{2,3},{3,2},{4,5},{5,4},{6,7},{7,6},{8,9},{9,8},{10,11... | collective-permute-start | bytes 1671176 | tf_op jit(solution)/shard_map/ppermute | solution.py:364
  532.2 22.8 %collective-permute-start.60 = (bf16[17,16,512]{2,1,0:T(8,128)(2,1)S(1)}, bf16[17,16,512]{2,1,0:T(8,128)(2,1)S(1)}, u32[]{:S(2)}, u32[]{:S(2)}) collective-permute-start(bf16[17,16,512]{2,1,0:T(8,128)(2,1)S(1)} %slice.593), channel_id=1, source_target_pairs={{0,16},{2,18},{4,20},{6,22},{8,24},{10,26},{12,28},{14,30},{16,0},... | collective-permute-start | bytes 835592 | tf_op jit(solution)/shard_map/ppermute | solution.py:364
  532.3 31.3 %collective-permute-start.76 = (bf16[17,16,512]{2,1,0:T(8,128)(2,1)S(1)}, bf16[17,16,512]{2,1,0:T(8,128)(2,1)S(1)}, u32[]{:S(2)}, u32[]{:S(2)}) collective-permute-start(bf16[17,16,512]{2,1,0:T(8,128)(2,1)S(1)} %fusion), channel_id=1, source_target_pairs={{0,1},{1,0},{2,3},{3,2},{4,5},{5,4},{6,7},{7,6},{8,9},{9,8},{10,11... | collective-permute-start | bytes 835592 | tf_op jit(solution)/shard_map/ppermute | solution.py:364
  550.6 27.9 %collective-permute-start.14 = (bf16[17,32,384]{2,1,0:T(8,128)(2,1)S(1)}, bf16[17,32,384]{2,1,0:T(8,128)(2,1)S(1)}, u32[]{:S(2)}, u32[]{:S(2)}) collective-permute-start(bf16[17,32,384]{2,1,0:T(8,128)(2,1)S(1)} %get-tuple-element.86), channel_id=1, source_target_pairs={{0,1},{1,0},{2,3},{3,2},{4,5},{5,4},{6,7},{7,6},{8,9},{9,8},{10,11... | collective-permute-start | bytes 1253384 | tf_op jit(solution)/shard_map/ppermute | solution.py:364
  552.1 21.4 %collective-permute-start.45 = (bf16[17,16,512]{2,1,0:T(8,128)(2,1)S(1)}, bf16[17,16,512]{2,1,0:T(8,128)(2,1)S(1)}, u32[]{:S(2)}, u32[]{:S(2)}) collective-permute-start(bf16[17,16,512]{2,1,0:T(8,128)(2,1)S(1)} %slice.594), channel_id=1, source_target_pairs={{0,16},{2,18},{4,20},{6,22},{8,24},{10,26},{12,28},{14,30},{16,0},... | collective-permute-start | bytes 835592 | tf_op jit(solution)/shard_map/ppermute | solution.py:364
  555.2 23.3 %collective-permute-start.61 = (bf16[17,16,512]{2,1,0:T(8,128)(2,1)S(1)}, bf16[17,16,512]{2,1,0:T(8,128)(2,1)S(1)}, u32[]{:S(2)}, u32[]{:S(2)}) collective-permute-start(bf16[17,16,512]{2,1,0:T(8,128)(2,1)S(1)} %fusion.1), channel_id=1, source_target_pairs={{0,1},{1,0},{2,3},{3,2},{4,5},{5,4},{6,7},{7,6},{8,9},{9,8},{10,11... | collective-permute-start | bytes 835592 | tf_op jit(solution)/shard_map/ppermute | solution.py:364
  (158 other events, 1502.2 us)
Sparse Core Ops, SparseCore 0:
  253.2 56.5 reduce-scatter.1
